TPU v7x, 256 devices: a whole 4x4x8 slice. The times are simulated.
256 devices in a mesh: row: 32 (over z, y_hi, core), col: 8 (over x, y_lo).
Axes of the slice: x: 4, y: 4 (y_hi: 2, y_lo: 2; y = y_hi * 2 + y_lo), z: 8, core: 2. Of those that a mesh axis runs over, the one named last changes fastest.
Arguments:
- inputs: bfloat16 [32, 8, 2, 128, 1024], P('row', 'col'), may hold values from -6 to 6
- targets: bfloat16 [32, 8, 2, 128, 1024], P('row', 'col'), may hold values from -6 to 6
- up_master: float32 [8, 1024, 2048], P('col', 'row'), may hold values from -6 to 6
- up_momentum: float32 [8, 1024, 2048], P('col', 'row'), may hold values from -0.75 to 0.75
- down_master: float32 [32, 2048, 1024], P('row', 'col'), may hold values from -6 to 6
- down_momentum: float32 [32, 2048, 1024], P('row', 'col'), may hold values from -0.75 to 0.75
Outputs:
- new_up: float32 [8, 1024, 2048], P('col', 'row')
- new_up_momentum: float32 [8, 1024, 2048], P('col', 'row')
- new_down: float32 [32, 2048, 1024], P('row', 'col')
- new_down_momentum: float32 [32, 2048, 1024], P('row', 'col')
All inputs are finite; a program needn't handle non-finite values.
Results may differ from a plain program's by a relative error of at most 0.015.
The roundings to bfloat16 on the way count: a program that leaves them out, or rounds other values in their place, can miss the bound.
Values may be sent and summed in bfloat16 or wider, within the bound.
No kernel may reach another device: no remote copies, remote signals or barrier semaphores. Data moves between devices by JAX's collectives and lax.ppermute only.
A program may use at most 128 MiB of HBM per device.

v0:
```python
import jax
import jax.numpy as jnp
from jax import lax
from jax.experimental import pallas as pl
from jax.experimental.pallas import tpu as pltpu
from jax.sharding import PartitionSpec as P

adam_rate = 0.05
beta_one = 0.9
beta_two = 0.95
adam_eps = 1e-06
decay_rate = 0.1
outer_rate = 0.7
outer_beta = 0.9
norm_eps = 1e-06

bf16 = jnp.bfloat16
f32 = jnp.float32

TOK, D, FFW = 128, 1024, 2048
BLK = 256
SEND, KEEP = 448, 512
EARLY, LATE = 768, 1280
width_scale = D ** (-0.5)
hidden_scale = FFW ** (-0.5)
ROOT = (2 / 3.141592653589793) ** 0.5


def swap_core(a):
    return lax.ppermute(a, "row", [(i, i ^ 1) for i in range(32)])


def swap_yh(a):
    return lax.ppermute(a, "row", [(i, i ^ 2) for i in range(32)])


def swap_both(a):
    return lax.ppermute(a, "row", [(i, i ^ 3) for i in range(32)])


def from_z(a):
    return lax.ppermute(a, "row", [(i, (i + (4 if i % 2 else -4)) % 32) for i in range(32)])


def to_z(a):
    return lax.ppermute(a, "row", [(i, (i + (-4 if i % 2 else 4)) % 32) for i in range(32)])


def swap_yl(a):
    return lax.ppermute(a, "col", [(i, i ^ 1) for i in range(8)])


def from_x(a, k):
    return lax.ppermute(a, "col", [(i, (i - 2 * k) % 8) for i in range(8)])


def up_order():
    own = [(0, 0, 0), (0, 1, 0), (0, 0, 1), (0, 1, 1)]
    side = [(4, 0, 0), (4, 1, 0)] + [(k, y, c) for k in (1, 2, 3) for _, y, c in own]
    other = [(-k, y, 1 - c) for k, y, c in side]
    return other, side, own


DOWN_ORDER = ((1, 1), (2, 1), (3, 1), (0, 1), (0, 0), (1, 0), (2, 0), (3, 0))


def after(*others):
    total = others[0][:16, :128]
    for o in others[1:]:
        total = total + o[:16, :128]
    return 0 * total


def hold(a, *others):
    return lax.dynamic_update_slice(a, a[:16, :128] + after(*others), (0, 0))


def gather(up, down, normed_t):
    own = [up, swap_yh(up), swap_core(up), swap_both(up)]
    c1, c3, d0 = from_x(down, 1), from_x(down, -1), swap_yl(down)
    one = from_z(jnp.concatenate(own, 0))
    one = hold(one, c1, c3)
    c2a, c2b = from_x(c1[:128], 1), from_x(c3[128:], -1)
    d1, d3 = from_x(d0, 1), from_x(d0, -1)
    two = from_z(one)
    two = hold(two, c2a, c2b, d0, normed_t[0])
    d2 = swap_yl(jnp.concatenate([c2a, c2b], 0))
    three = from_z(two)
    side = [from_z(three[:64]), one, two, three]
    both = swap_core(jnp.concatenate(side[1:3], 0))
    other = [swap_core(side[0]), both, swap_core(side[3])]
    return other, side, own, [d1, d2, d3, d0, down, c1, c2a, c2b, c3]


def add(*parts):
    total = parts[0].astype(f32)
    for p in parts[1:]:
        total = total + p.astype(f32)
    return total


def scatter(v_first, v_keep, v_early, late_change):
    u1, u2, u3 = v_early
    v_other, v_four = v_first
    got = swap_core(v_other)

    def side(at, mine, *more):
        return add(mine, got[at : at + mine.shape[0]], *more).astype(bf16)

    def wide(p):
        return jnp.pad(p, ((0, 128 - p.shape[0]), (0, FFW - p.shape[1])))

    r = to_z(side(0, v_four))
    u0, t0, t1, t2, t3 = late_change(r)
    p, m, w = from_x(u1, -1), from_x(u3, 1), swap_yl(u2)
    r = to_z(side(320, v_keep[2], wide(r), wide(after(u1))))
    u0 = add(u0, p, m).astype(bf16)
    t2 = add(t2, w).astype(bf16)
    r = to_z(side(192, v_keep[1], r, wide(after(u0, t2))))
    p, m, w = from_x(t2[:128], -1), from_x(t2[128:], 1), swap_yl(u0)
    t1 = add(t1, jnp.pad(p, ((0, 128), (0, 0)))).astype(bf16)
    t3 = add(t3, jnp.pad(m, ((128, 0), (0, 0)))).astype(bf16)
    r = to_z(side(64, v_keep[0], r, wide(after(t1, t3))))
    p, m = from_x(t1, -1), from_x(t3, 1)
    down = add(t0, w, p, m)
    wait = jnp.pad(after(p, m, w), ((0, 48), (0, FFW - 128)))
    away = add(v_keep[4], r[64:], wait).astype(bf16)
    both = add(v_keep[3], r[:64], swap_core(away))
    up = both[:32] + swap_yh(both[32:].astype(bf16)).astype(f32)
    return up, down


def hidden_place(k):
    col = lax.axis_index("col")
    x, yl = col // 2, col % 2
    dx, dyl = DOWN_ORDER[k]
    return ((x + dx) % 4) * 2 + (yl + dyl) % 2


def feature_place():
    row = lax.axis_index("row")
    z, yh, core = row // 4, (row // 2) % 2, row % 2
    sign = 1 - 2 * core
    other, side, own = up_order()
    return [
        ((z + sign * k + 8) % 8) * 4 + ((yh + y) % 2) * 2 + (core + c) % 2 for k, y, c in other + side + own
    ]


def dot(a, b, dims=((1,), (0,))):
    return lax.dot_general(a, b, (dims, ((), ())), preferred_element_type=f32)


def gelu(x):
    return 0.5 * x * (1.0 + jnp.tanh(ROOT * (x + 0.044715 * x * x * x)))


def gelu_slope(x):
    t = jnp.tanh(ROOT * (x + 0.044715 * x * x * x))
    return 0.5 * (1.0 + t) + 0.5 * x * (1.0 - t * t) * (ROOT * (1.0 + 3 * 0.044715 * x * x))


def first_weight(start, raw, scale):
    part = raw / (jnp.abs(raw) + adam_eps / scale)
    return (1 - adam_rate * decay_rate) * start.astype(f32) - adam_rate * part


def change_of(start, one, two, scale):
    eps = adam_eps / scale
    left = 1 - adam_rate * decay_rate
    ca, cb = (1 - beta_one) * beta_one / (1 - beta_one**2), (1 - beta_one) / (1 - beta_one**2)
    cc, cd = (1 - beta_two) * beta_two / (1 - beta_two**2), (1 - beta_two) / (1 - beta_two**2)
    part_one = one / ((jnp.abs(one) + eps) * (1 / (adam_rate * left)))
    square = one * one + (cd / cc) * (two * two)
    size = square * lax.rsqrt(jnp.maximum(square, 1e-36))
    root = cc**0.5
    part_two = (one + (cb / ca) * two) / ((size + eps / root) * (root / (adam_rate * ca)))
    return (part_one + part_two + (1 - left * left) * start.astype(f32)).astype(bf16)


def prepare(x):
    def kernel(x_ref, n_ref, t_ref):
        lane = lax.broadcasted_iota(jnp.int32, (1, D), 1)
        place = lane
        for i, first in enumerate(feature_place()):
            place = jnp.where(lane // 32 == i, first * 32 + lane % 32, place)
        feats = x_ref[...].astype(f32)
        square_mean = jnp.mean(feats * feats, axis=-1, keepdims=True)
        normed = (feats * lax.rsqrt(square_mean + norm_eps)).astype(bf16).reshape(2 * TOK, D)
        for j in range(D // BLK):
            cols = slice(j * BLK, j * BLK + BLK)
            order = lax.broadcasted_iota(jnp.int32, (D, BLK), 0) == place[:, cols]
            part = dot(normed, order.astype(f32).astype(bf16))
            for t in range(2):
                rows = part[t * TOK : t * TOK + TOK]
                n_ref[t, :, cols] = rows.astype(bf16)
                t_ref[t, cols, :] = rows.T.astype(bf16)

    return pl.pallas_call(
        kernel,
        out_shape=(
            jax.ShapeDtypeStruct((2, TOK, D), bf16),
            jax.ShapeDtypeStruct((2, D, TOK), bf16),
        ),
        compiler_params=pltpu.CompilerParams(vmem_limit_bytes=12 * 1024 * 1024),
        cost_estimate=pl.CostEstimate(flops=2 * 10**8, bytes_accessed=2**21, transcendentals=0),
        name="prepare",
    )(x)


def inner_kernel(up_pieces, down_pieces, *refs):
    count = len(up_pieces) + len(down_pieces)
    n_ref, nt_ref, x_ref, t_ref = refs[:4]
    pieces = refs[4 : 4 + count]
    act_ref, g_ref, gp_ref, send_ref, keep_ref, early_ref, late_ref = refs[4 + count : 11 + count]
    su, sd, w1u, w1d, pre_ref, place_ref, sem, out_sem = refs[11 + count :]

    up_copies, down_copies = [], []
    for i, (start, rows, at) in enumerate(up_pieces):
        up_copies.append(
            pltpu.make_async_copy(pieces[i].at[pl.ds(start, rows)], su.at[pl.ds(at, rows)], sem.at[i])
        )
    for j, (start, rows, at) in enumerate(down_pieces):
        i = j + len(up_pieces)
        down_copies.append(
            pltpu.make_async_copy(pieces[i].at[pl.ds(start, rows)], sd.at[pl.ds(at, rows)], sem.at[i])
        )
    for c in up_copies + down_copies:
        c.start()
    for k in range(8):
        place_ref[k] = hidden_place(k)
    for c in up_copies:
        c.wait()

    def columns(k):
        return pl.ds(pl.multiple_of(place_ref[k] * BLK, BLK), BLK)

    def slot(k):
        return pl.ds(pl.multiple_of(k * BLK, BLK), BLK)

    @pl.loop(0, 8, unroll=2)
    def _(k):
        pre = dot(n_ref[0], su[:, columns(k)]) * width_scale
        pre_ref[:, slot(k)] = pre
        act_ref[0, :, slot(k)] = gelu(pre).astype(bf16)

    for c in down_copies:
        c.wait()
    outs = [
        pltpu.make_async_copy(su.at[pl.ds(0, D - KEEP)], send_ref, out_sem.at[0]),
        pltpu.make_async_copy(su.at[pl.ds(D - KEEP, KEEP)], keep_ref, out_sem.at[1]),
        pltpu.make_async_copy(sd.at[pl.ds(0, EARLY)], early_ref, out_sem.at[2]),
        pltpu.make_async_copy(sd.at[pl.ds(EARLY, LATE)], late_ref, out_sem.at[3]),
    ]
    for c in outs:
        c.start()

    def grad_out(t, weight):
        @pl.loop(0, D // BLK, unroll=2)
        def _(j):
            outval = dot(act_ref[t], weight[:, slot(j)]) * hidden_scale
            resid = x_ref[t, :, slot(j)].astype(f32) + outval - t_ref[t, :, slot(j)].astype(f32)
            g_ref[t, :, slot(j)] = (resid * (1.0 / TOK)).astype(bf16)

    def grad_pre(t, weight):
        @pl.loop(0, 8, unroll=2)
        def _(k):
            grad_act = dot(g_ref[t], weight[slot(k), :], ((1,), (1,))) * hidden_scale
            gp_ref[t, :, columns(k)] = (grad_act * gelu_slope(pre_ref[:, slot(k)])).astype(bf16)

    grad_out(0, sd)
    grad_pre(0, sd)

    @pl.loop(0, 8, unroll=2)
    def _(k):
        raw = dot(nt_ref[0], gp_ref[0, :, columns(k)])
        w1u[...] = first_weight(su[:, columns(k)], raw, width_scale).astype(bf16)
        raw = dot(act_ref[0, :, slot(k)], g_ref[0], ((0,), (0,)))
        w1d[slot(k), :] = first_weight(sd[slot(k), :], raw, hidden_scale).astype(bf16)
        pre = dot(n_ref[1], w1u[...]) * width_scale
        pre_ref[:, slot(k)] = pre
        act_ref[1, :, slot(k)] = gelu(pre).astype(bf16)

    grad_out(1, w1d)
    grad_pre(1, w1d)
    for c in outs:
        c.wait()


def inner_steps(normed, normed_t, x, t, up_pieces, down_pieces):
    vmem, hbm = pl.BlockSpec(memory_space=pltpu.VMEM), pl.BlockSpec(memory_space=pl.ANY)
    far = pl.BlockSpec(memory_space=pl.ANY)
    pieces = [p[0] for p in up_pieces + down_pieces]

    def kernel(*refs):
        inner_kernel([p[1:] for p in up_pieces], [p[1:] for p in down_pieces], *refs)

    return pl.pallas_call(
        kernel,
        out_shape=(
            jax.ShapeDtypeStruct((2, TOK, FFW), bf16),
            jax.ShapeDtypeStruct((2, TOK, D), bf16),
            jax.ShapeDtypeStruct((2, TOK, FFW), bf16),
            jax.ShapeDtypeStruct((D - KEEP, FFW), bf16),
            jax.ShapeDtypeStruct((KEEP, FFW), bf16),
            jax.ShapeDtypeStruct((EARLY, D), bf16),
            jax.ShapeDtypeStruct((LATE, D), bf16),
        ),
        in_specs=[vmem] * 4 + [far] * len(pieces),
        out_specs=(vmem, vmem, vmem, hbm, hbm, hbm, hbm),
        scratch_shapes=[
            pltpu.VMEM((D, FFW), bf16),
            pltpu.VMEM((FFW, D), bf16),
            pltpu.VMEM((D, BLK), bf16),
            pltpu.VMEM((FFW, D), bf16),
            pltpu.VMEM((TOK, FFW), f32),
            pltpu.SMEM((8,), jnp.int32),
            pltpu.SemaphoreType.DMA((len(pieces),)),
            pltpu.SemaphoreType.DMA((4,)),
        ],
        compiler_params=pltpu.CompilerParams(vmem_limit_bytes=20 * 1024 * 1024),
        cost_estimate=pl.CostEstimate(flops=5 * 10**9, bytes_accessed=24 * 2**20, transcendentals=0),
        name="inner_steps",
    )(normed, normed_t, x, t, *pieces)


def up_change(start, normed_t, grad_pre, first, parts):
    rows = start.shape[0]
    wide = 2 * BLK

    def kernel(s_ref, n_ref, g_ref, *o_refs):
        one = dot(n_ref[0, pl.ds(first, rows)], g_ref[0])
        two = dot(n_ref[1, pl.ds(first, rows)], g_ref[1])
        change = change_of(s_ref[...], one, two, width_scale)
        at = 0
        for part, o_ref in zip(parts, o_refs):
            o_ref[...] = change[at : at + part]
            at += part

    return pl.pallas_call(
        kernel,
        grid=(FFW // wide,),
        out_shape=tuple(jax.ShapeDtypeStruct((part, FFW), bf16) for part in parts),
        in_specs=[
            pl.BlockSpec((rows, wide), lambda j: (0, j)),
            pl.BlockSpec((2, D, TOK), lambda j: (0, 0, 0)),
            pl.BlockSpec((2, TOK, wide), lambda j: (0, 0, j)),
        ],
        out_specs=tuple(pl.BlockSpec((part, wide), lambda j: (0, j)) for part in parts),
        compiler_params=pltpu.CompilerParams(vmem_limit_bytes=10 * 1024 * 1024),
        cost_estimate=pl.CostEstimate(flops=4 * rows * TOK * FFW, bytes_accessed=4 * rows * FFW, transcendentals=0),
        name="up_change",
    )(start, normed_t, grad_pre)


def down_change(start, act, grad_out, first, *awaited):
    rows = start.shape[0]

    def kernel(s_ref, a_ref, g_ref, *refs):
        o_refs = refs[len(awaited) :]
        one = dot(a_ref[0, :, pl.ds(first, rows)], g_ref[0], ((0,), (0,)))
        two = dot(a_ref[1, :, pl.ds(first, rows)], g_ref[1], ((0,), (0,)))
        change = change_of(s_ref[...], one, two, hidden_scale)
        for i, o_ref in enumerate(o_refs):
            o_ref[...] = change[BLK * i : BLK * i + BLK]

    return pl.pallas_call(
        kernel,
        grid=(D // BLK,),
        out_shape=(jax.ShapeDtypeStruct((BLK, D), bf16),) * (rows // BLK),
        in_specs=[
            pl.BlockSpec((rows, BLK), lambda j: (0, j)),
            pl.BlockSpec((2, TOK, FFW), lambda j: (0, 0, 0)),
            pl.BlockSpec((2, TOK, BLK), lambda j: (0, 0, j)),
        ]
        + [pl.BlockSpec(memory_space=pl.ANY)] * len(awaited),
        out_specs=(pl.BlockSpec((BLK, BLK), lambda j: (0, j)),) * (rows // BLK),
        compiler_params=pltpu.CompilerParams(vmem_limit_bytes=10 * 1024 * 1024),
        cost_estimate=pl.CostEstimate(flops=4 * rows * TOK * D, bytes_accessed=4 * rows * D, transcendentals=0),
        name="down_change",
    )(start, act, grad_out, *awaited)


def local(inputs, targets, up_master, up_momentum, down_master, down_momentum):
    x, t = inputs[0, 0], targets[0, 0]
    rel, rel_t = prepare(x)
    other, side, own, down_blocks = gather(
        up_master[0].astype(bf16), down_master[0].astype(bf16), rel_t
    )
    down_pieces, at = [], 0
    for a in down_blocks:
        down_pieces.append((a, 0, a.shape[0], at))
        at += a.shape[0]
    up_pieces, at = [], 0
    for a in other + side + own:
        up_pieces.append((a, 0, a.shape[0], at))
        at += a.shape[0]

    act, grad_out, grad_pre, up_other, up_keep, down_early, down_late = inner_steps(
        rel, rel_t, x, t, up_pieces, down_pieces
    )
    up_sum, down_sum = scatter(
        up_change(up_other, rel_t, grad_pre, 0, (SEND, 64)),
        up_change(up_keep, rel_t, grad_pre, D - KEEP, (128, 128, 128, 64, 64)),
        down_change(down_early, act, grad_out, 0),
        lambda r: down_change(down_late, act, grad_out, EARLY, r),
    )
    up_avg, down_avg = up_sum / 32, down_sum / 8
    new_up_momentum = outer_beta * up_momentum + up_avg[None]
    new_up = up_master - outer_rate * (up_avg[None] + outer_beta * new_up_momentum)
    new_down_momentum = outer_beta * down_momentum + down_avg[None]
    new_down = down_master - outer_rate * (down_avg[None] + outer_beta * new_down_momentum)
    return (new_up, new_up_momentum, new_down, new_down_momentum)


def solution(mesh):
    in_specs = (
        P("row", "col", None, None, None),
        P("row", "col", None, None, None),
        P("col", "row", None),
        P("col", "row", None),
        P("row", "col", None),
        P("row", "col", None),
    )
    out_specs = (
        P("col", "row", None),
        P("col", "row", None),
        P("row", "col", None),
        P("row", "col", None),
    )
    return jax.shard_map(local, mesh=mesh, in_specs=in_specs, out_specs=out_specs, check_vma=False)
```

profile of v0, /device:TPU:1, one launch (start us, length us, event | category | flops | bytes accessed | tf_op | source)
XLA Modules:
  0.0 137.6 jit_solution(4702491022267773405)
XLA Ops:
  1.6 4.4 %collective-permute-start.2 = (bf16[32,2048]{1,0:T(8,128)(2,1)S(1)}, bf16[32,2048]{1,0:T(8,128)(2,1)S(1)}, u32[]{:S(2)}, u32[]{:S(2)}) collective-permute-start(bf16[32,2048]{1,0:T(8,128)(2,1)S(1)} %convert_bitcast_fusion.1.refs_11_), channel_id=1, source_target_pairs={{0,24},{8,16},{16,8},{24,0},{32,56},{40,48},{48,40},{56,32},{64,88... | collective-permute-start | bytes 393224 | tf_op jit(solution)/shard_map/ppermute | solution.py:38
  6.0 1.8 %collective-permute-start = (bf16[32,2048]{1,0:T(8,128)(2,1)S(1)}, bf16[32,2048]{1,0:T(8,128)(2,1)S(1)}, u32[]{:S(2)}, u32[]{:S(2)}) collective-permute-start(bf16[32,2048]{1,0:T(8,128)(2,1)S(1)} %convert_bitcast_fusion.1.refs_11_), channel_id=1, source_target_pairs={{0,16},{8,24},{16,0},{24,8},{32,48},{40,56},{48,32},{56,40},{64,80... | collective-permute-start | bytes 393224 | tf_op jit(solution)/shard_map/ppermute | solution.py:34
  7.8 1.3 convert_bitcast_fusion.refs_19_
  9.2 2.7 %collective-permute-start.4 = (bf16[256,1024]{1,0:T(8,128)(2,1)S(1)}, bf16[256,1024]{1,0:T(8,128)(2,1)S(1)}, u32[]{:S(2)}, u32[]{:S(2)}) collective-permute-start(bf16[256,1024]{1,0:T(8,128)(2,1)S(1)} %convert_bitcast_fusion.refs_19_), channel_id=1, source_target_pairs={{0,6},{1,7},{2,0},{3,1},{4,2},{5,3},{6,4},{7,5},{8,14},{9,15},{10,... | collective-permute-start | bytes 1572872 | tf_op jit(solution)/shard_map/ppermute | solution.py:54
  12.5 1.4 %collective-permute-start.3 = (bf16[128,2048]{1,0:T(8,128)(2,1)S(1)}, bf16[128,2048]{1,0:T(8,128)(2,1)S(1)}, u32[]{:S(2)}, u32[]{:S(2)}) collective-permute-start(bf16[128,2048]{1,0:T(8,128)(2,1)S(1)} %pad_maximum_fusion.1), channel_id=1, source_target_pairs={{0,224},{8,40},{16,240},{24,56},{32,0},{40,72},{48,16},{56,88},{64... | collective-permute-start | bytes 1572872 | tf_op jit(solution)/shard_map/ppermute | solution.py:42
  13.9 1.9 %collective-permute-start.9 = (bf16[256,1024]{1,0:T(8,128)(2,1)S(1)}, bf16[256,1024]{1,0:T(8,128)(2,1)S(1)}, u32[]{:S(2)}, u32[]{:S(2)}) collective-permute-start(bf16[256,1024]{1,0:T(8,128)(2,1)S(1)} %convert_bitcast_fusion.refs_19_), channel_id=1, source_target_pairs={{0,1},{1,0},{2,3},{3,2},{4,5},{5,4},{6,7},{7,6},{8,9},{9,8},{10,11... | collective-permute-start | bytes 1572872 | tf_op jit(solution)/shard_map/ppermute | solution.py:50
  15.7 7.3 %collective-permute-done.5.refs_23_ = bf16[256,1024]{1,0:T(8,128)(2,1)S(1)} collective-permute-done((bf16[256,1024]{1,0:T(8,128)(2,1)S(1)}, bf16[256,1024]{1,0:T(8,128)(2,1)S(1)}, u32[]{:S(2)}, u32[]{:S(2)}) %collective-permute-start.5) | collective-permute-done | bytes 524320 | tf_op jit(solution)/shard_map/ppermute | solution.py:54
  23.1 1.3 collective-permute-done.3
  25.8 1.5 %collective-permute-start.7 = (bf16[128,1024]{1,0:T(8,128)(2,1)S(1)}, bf16[128,1024]{1,0:T(8,128)(2,1)S(1)}, u32[]{:S(2)}, u32[]{:S(2)}) collective-permute-start(bf16[128,1024]{1,0:T(8,128)(2,1)S(1)} %slice.127), channel_id=1, source_target_pairs={{0,6},{1,7},{2,0},{3,1},{4,2},{5,3},{6,4},{7,5},{8,14},{9,15},{10,... | collective-permute-start | bytes 786440 | tf_op jit(solution)/shard_map/ppermute | solution.py:54
  28.5 2.5 %collective-permute-done.8.refs_22_ = bf16[128,1024]{1,0:T(8,128)(2,1)S(1)} collective-permute-done((bf16[128,1024]{1,0:T(8,128)(2,1)S(1)}, bf16[128,1024]{1,0:T(8,128)(2,1)S(1)}, u32[]{:S(2)}, u32[]{:S(2)}) %collective-permute-start.8) | collective-permute-done | bytes 262176 | tf_op jit(solution)/shard_map/ppermute | solution.py:54
  31.4 2.5 %collective-permute-done.6 = bf16[128,2048]{1,0:T(8,128)(2,1)S(1)} collective-permute-done((bf16[128,2048]{1,0:T(8,128)(2,1)S(1)}, bf16[128,2048]{1,0:T(8,128)(2,1)S(1)}, u32[]{:S(2)}, u32[]{:S(2)}) %collective-permute-start.6) | collective-permute-done | bytes 524320 | tf_op jit(solution)/shard_map/ppermute | solution.py:42
  34.1 6.6 %collective-permute-start.13 = (bf16[256,2048]{1,0:T(8,128)(2,1)S(1)}, bf16[256,2048]{1,0:T(8,128)(2,1)S(1)}, u32[]{:S(2)}, u32[]{:S(2)}) collective-permute-start(bf16[256,2048]{1,0:T(8,128)(2,1)S(1)} %pad_maximum_fusion), channel_id=1, source_target_pairs={{0,8},{8,0},{16,24},{24,16},{32,40},{40,32},{48,56},{56,48},{64,72... | collective-permute-start | bytes 3145736 | tf_op jit(solution)/shard_map/ppermute | solution.py:30
  40.8 2.3 %collective-permute-start.15 = (bf16[256,1024]{1,0:T(8,128)(2,1)S(1)}, bf16[256,1024]{1,0:T(8,128)(2,1)S(1)}, u32[]{:S(2)}, u32[]{:S(2)}) collective-permute-start(bf16[256,1024]{1,0:T(8,128)(2,1)S(1)} %collective-permute-done.9.refs_18_), channel_id=1, source_target_pairs={{0,6},{1,7},{2,0},{3,1},{4,2},{5,3},{6,4},{7,5},{8,14},{9,15},{10,... | collective-permute-start | bytes 1572872 | tf_op jit(solution)/shard_map/ppermute | solution.py:54
  45.2 5.9 %collective-permute-start.14 = (bf16[128,2048]{1,0:T(8,128)(2,1)S(1)}, bf16[128,2048]{1,0:T(8,128)(2,1)S(1)}, u32[]{:S(2)}, u32[]{:S(2)}) collective-permute-start(bf16[128,2048]{1,0:T(8,128)(2,1)S(1)} %collective-permute-done.10.refs_10_), channel_id=1, source_target_pairs={{0,8},{8,0},{16,24},{24,16},{32,40},{40,32},{48,56},{56,48},{64,72... | collective-permute-start | bytes 1572872 | tf_op jit(solution)/shard_map/ppermute | solution.py:30
  51.1 5.1 %collective-permute-start.12 = (bf16[64,2048]{1,0:T(8,128)(2,1)S(1)}, bf16[64,2048]{1,0:T(8,128)(2,1)S(1)}, u32[]{:S(2)}, u32[]{:S(2)}) collective-permute-start(bf16[64,2048]{1,0:T(8,128)(2,1)S(1)} %collective-permute-done.11.refs_7_), channel_id=1, source_target_pairs={{0,8},{8,0},{16,24},{24,16},{32,40},{40,32},{48,56},{56,48},{64,72... | collective-permute-start | bytes 786440 | tf_op jit(solution)/shard_map/ppermute | solution.py:30
  57.4 16.7 %inner_steps.1 = (bf16[2,128,2048]{2,1,0:T(8,128)(2,1)S(1)}, bf16[2,128,1024]{2,1,0:T(8,128)(2,1)S(1)}, bf16[2,128,2048]{2,1,0:T(8,128)(2,1)S(1)}, bf16[512,2048...) custom-call(bf16[2,128,1024]{2,1,0:T(8,128)(2,1)S(1)} %get-tuple-ele, ...), custom_call_target="tpu_custom_call" | custom-call | flops 5000000000 | bytes 25165824 | tf_op jit(solution)/shard_map/inner_steps/pallas_call | solution.py:298
  74.1 4.2 %up_change.3 = (bf16[448,2048]{1,0:T(8,128)(2,1)S(1)}, bf16[64,2048]{1,0:T(8,128)(2,1)S(1)}) custom-call(bf16[512,2048]{1,0:T(8,128)(2,1)S(1)} %get-tuple-element.34.s_ref, bf16[2,1024,128]{2,1,0:T(8,128)(2,1)S(1)} %get-tuple-element.29.refs_1_.n_ref, bf16[2,128,2048]{2,1,0:T(8,128)(2,1)S(1)} %get-tuple-element.31.g_ref), custom_call_target="tpu_custom_call" | custom-call | flops 536870912 | bytes 4194304 | tf_op jit(solution)/shard_map/up_change/pallas_call | solution.py:340
  78.8 3.6 %down_change.2 = (bf16[256,1024]{1,0:T(8,128)(2,1)S(1)}, bf16[256,1024]{1,0:T(8,128)(2,1)S(1)}, bf16[256,1024]{1,0:T(8,128)(2,1)S(1)}) custom-call(bf16[768,1024]{1,0:T(8,128)(2,1)S(1)} %get-tuple-element.39.s_ref, bf16[2,128,2048]{2,1,0:T(8,128)(2,1)S(1)} %get-tuple-element.40.a_ref, bf16[2,128,1024]{2,1,0:T(8,128)(2,1)S(1)} %get-tuple-element.41.g_ref), custom_call_target="tpu_custom_call" | custom-call | flops 402653184 | bytes 3145728 | tf_op jit(solution)/shard_map/down_change/pallas_call | solution.py:367
  83.6 1.3 collective-permute-start.23
  85.2 3.1 %collective-permute-start.19 = (bf16[64,2048]{1,0:T(8,128)(2,1)S(1)}, bf16[64,2048]{1,0:T(8,128)(2,1)S(1)}, u32[]{:S(2)}, u32[]{:S(2)}) collective-permute-start(bf16[64,2048]{1,0:T(8,128)(2,1)S(1)} %add_convert_fusion.8), channel_id=1, source_target_pairs={{0,32},{8,232},{16,48},{24,248},{32,64},{40,8},{48,80},{56,24},{64... | collective-permute-start | bytes 786440 | tf_op jit(solution)/shard_map/ppermute | solution.py:46
  88.3 4.3 %up_change.2 = (bf16[128,2048]{1,0:T(8,128)(2,1)S(1)}, bf16[128,2048]{1,0:T(8,128)(2,1)S(1)}, bf16[128,2048]{1,0:T(8,128)(2,1)S(1)}, bf16[64,2048]{1,0:T(8,128)(2,1)S(1)}, bf16[64,2048]{1,0:T(8,128)(2,1)S(1)}) custom-call(bf16[512,2048]{1,0:T(8,128)(2,1)S(1)} %get-tuple-element.30.s_ref, bf16[2,1024,128]{2,1,0:T(8,128)(2,1)S(1)} %get-tuple-element.29.refs_1_.n_ref, ...), custom_call_target="tpu_custom_call" | custom-call | flops 536870912 | bytes 4194304 | tf_op jit(solution)/shard_map/up_change/pallas_call | solution.py:340
  92.8 2.7 %collective-permute-start.20 = (bf16[128,2048]{1,0:T(8,128)(2,1)S(1)}, bf16[128,2048]{1,0:T(8,128)(2,1)S(1)}, u32[]{:S(2)}, u32[]{:S(2)}) collective-permute-start(bf16[128,2048]{1,0:T(8,128)(2,1)S(1)} %add_convert_fusion.6), channel_id=1, source_target_pairs={{0,32},{8,232},{16,48},{24,248},{32,64},{40,8},{48,80},{56,24},{64... | collective-permute-start | bytes 1572872 | tf_op jit(solution)/shard_map/ppermute | solution.py:46
  95.5 5.4 %down_change.3 = (bf16[256,1024]{1,0:T(8,128)(2,1)S(1)}, bf16[256,1024]{1,0:T(8,128)(2,1)S(1)}, bf16[256,1024]{1,0:T(8,128)(2,1)S(1)}, bf16[256,1024]{1,0:T(8,128)(2,1)S(1)}, bf16[256,1024]{1,0:T(8,128)(2,1)S(1)}) custom-call(bf16[1280,1024]{1,0:T(8,128)(2,1)S(1)} %get-tuple-element.43.s_ref, bf16[2,128,2048]{2,1,0:T(8,128)(2,1)S(1)} %get-tuple-element.40.a_ref, ...), custom_call_target="tpu_custom_call" | custom-call | flops 671088640 | bytes 5242880 | tf_op jit(solution)/shard_map/down_change/pallas_call | solution.py:367
  101.3 2.8 %collective-permute-start.26 = (bf16[128,1024]{1,0:T(8,128)(2,1)S(1)}, bf16[128,1024]{1,0:T(8,128)(2,1)S(1)}, u32[]{:S(2)}, u32[]{:S(2)}) collective-permute-start(bf16[128,1024]{1,0:T(8,128)(2,1)S(1)} %get-tuple-element.57), channel_id=1, source_target_pairs={{0,6},{1,7},{2,0},{3,1},{4,2},{5,3},{6,4},{7,5},{8,14},{9,15},{10,... | collective-permute-start | bytes 786440 | tf_op jit(solution)/shard_map/ppermute | solution.py:54
  105.1 4.6 %collective-permute-done.26 = bf16[128,1024]{1,0:T(8,128)(2,1)S(1)} collective-permute-done((bf16[128,1024]{1,0:T(8,128)(2,1)S(1)}, bf16[128,1024]{1,0:T(8,128)(2,1)S(1)}, u32[]{:S(2)}, u32[]{:S(2)}) %collective-permute-start.26) | collective-permute-done | bytes 262176 | tf_op jit(solution)/shard_map/ppermute | solution.py:54
  109.8 3.5 %collective-permute-start.29 = (bf16[256,1024]{1,0:T(8,128)(2,1)S(1)}, bf16[256,1024]{1,0:T(8,128)(2,1)S(1)}, u32[]{:S(2)}, u32[]{:S(2)}) collective-permute-start(bf16[256,1024]{1,0:T(8,128)(2,1)S(1)} %add_convert_fusion.1), channel_id=1, source_target_pairs={{0,6},{1,7},{2,0},{3,1},{4,2},{5,3},{6,4},{7,5},{8,14},{9,15},{10,... | collective-permute-start | bytes 1572872 | tf_op jit(solution)/shard_map/ppermute | solution.py:54
  114.6 3.5 %collective-permute-done.30 = bf16[256,1024]{1,0:T(8,128)(2,1)S(1)} collective-permute-done((bf16[256,1024]{1,0:T(8,128)(2,1)S(1)}, bf16[256,1024]{1,0:T(8,128)(2,1)S(1)}, u32[]{:S(2)}, u32[]{:S(2)}) %collective-permute-start.30) | collective-permute-done | bytes 524320 | tf_op jit(solution)/shard_map/ppermute | solution.py:50
  118.1 6.5 %collective-permute-done.29 = bf16[256,1024]{1,0:T(8,128)(2,1)S(1)} collective-permute-done((bf16[256,1024]{1,0:T(8,128)(2,1)S(1)}, bf16[256,1024]{1,0:T(8,128)(2,1)S(1)}, u32[]{:S(2)}, u32[]{:S(2)}) %collective-permute-start.29) | collective-permute-done | bytes 524320 | tf_op jit(solution)/shard_map/ppermute | solution.py:54
  124.6 3.3 %collective-permute-done.28 = bf16[256,1024]{1,0:T(8,128)(2,1)S(1)} collective-permute-done((bf16[256,1024]{1,0:T(8,128)(2,1)S(1)}, bf16[256,1024]{1,0:T(8,128)(2,1)S(1)}, u32[]{:S(2)}, u32[]{:S(2)}) %collective-permute-start.28) | collective-permute-done | bytes 524320 | tf_op jit(solution)/shard_map/ppermute | solution.py:54
  130.4 2.7 %collective-permute-start.32 = (bf16[32,2048]{1,0:T(8,128)(2,1)S(1)}, bf16[32,2048]{1,0:T(8,128)(2,1)S(1)}, u32[]{:S(2)}, u32[]{:S(2)}) collective-permute-start(bf16[32,2048]{1,0:T(8,128)(2,1)S(1)} %slice.206), channel_id=1, source_target_pairs={{0,16},{8,24},{16,0},{24,8},{32,48},{40,56},{48,32},{56,40},{64,80... | collective-permute-start | bytes 393224 | tf_op jit(solution)/shard_map/ppermute | solution.py:34
  133.1 1.9 %fusion.1 = (f32[1,256,1024]{2,1,0:T(8,128)}, f32[1,256,1024]{2,1,0:T(8,128)}) fusion(f32[1,256,1024]{2,1,0:T(8,128)S(1)} %copy-done.2, bf16[256,1024]{1,0:T(8,128)(2,1)S(1)} %collective-permute-done.29, bf16[256,1024]{1,0:T(8,128)(2,1)S(1)} %collective-permute-done.28, bf16[256,1024]{1,0:T(8,128)(2,1)S(1)} %collective-permute-done.30, ...), kind=kLoop, calls=%fused_computation.4 | loop fusion | flops 3670016 | bytes 6291456 | tf_op jit(solution)/shard_map/sub | solution.py:412
  135.0 1.7 %collective-permute-done.32 = bf16[32,2048]{1,0:T(8,128)(2,1)S(1)} collective-permute-done((bf16[32,2048]{1,0:T(8,128)(2,1)S(1)}, bf16[32,2048]{1,0:T(8,128)(2,1)S(1)}, u32[]{:S(2)}, u32[]{:S(2)}) %collective-permute-start.32) | collective-permute-done | bytes 131104 | tf_op jit(solution)/shard_map/ppermute | solution.py:34
  (80 shorter events, 16.3 us)
Async XLA Ops:
  1.6 10.2 %collective-permute-start.2 = (bf16[32,2048]{1,0:T(8,128)(2,1)S(1)}, bf16[32,2048]{1,0:T(8,128)(2,1)S(1)}, u32[]{:S(2)}, u32[]{:S(2)}) collective-permute-start(bf16[32,2048]{1,0:T(8,128)(2,1)S(1)} %convert_bitcast_fusion.1.refs_11_), channel_id=1, source_target_pairs={{0,24},{8,16},{16,8},{24,0},{32,56},{40,48},{48,40},{56,32},{64,88... | collective-permute-start | bytes 393224 | tf_op jit(solution)/shard_map/ppermute | solution.py:38
  6.0 5.9 %collective-permute-start.1 = (bf16[32,2048]{1,0:T(8,128)(2,1)S(1)}, bf16[32,2048]{1,0:T(8,128)(2,1)S(1)}, u32[]{:S(2)}, u32[]{:S(2)}) collective-permute-start(bf16[32,2048]{1,0:T(8,128)(2,1)S(1)} %convert_bitcast_fusion.1.refs_11_), channel_id=1, source_target_pairs={{0,8},{8,0},{16,24},{24,16},{32,40},{40,32},{48,56},{56,48},{64,72... | collective-permute-start | bytes 393224 | tf_op jit(solution)/shard_map/ppermute | solution.py:30
  6.0 6.4 %collective-permute-start = (bf16[32,2048]{1,0:T(8,128)(2,1)S(1)}, bf16[32,2048]{1,0:T(8,128)(2,1)S(1)}, u32[]{:S(2)}, u32[]{:S(2)}) collective-permute-start(bf16[32,2048]{1,0:T(8,128)(2,1)S(1)} %convert_bitcast_fusion.1.refs_11_), channel_id=1, source_target_pairs={{0,16},{8,24},{16,0},{24,8},{32,48},{40,56},{48,32},{56,40},{64,80... | collective-permute-start | bytes 393224 | tf_op jit(solution)/shard_map/ppermute | solution.py:34
  9.1 13.9 %collective-permute-start.5 = (bf16[256,1024]{1,0:T(8,128)(2,1)S(1)}, bf16[256,1024]{1,0:T(8,128)(2,1)S(1)}, u32[]{:S(2)}, u32[]{:S(2)}) collective-permute-start(bf16[256,1024]{1,0:T(8,128)(2,1)S(1)} %convert_bitcast_fusion.refs_19_), channel_id=1, source_target_pairs={{0,2},{1,3},{2,4},{3,5},{4,6},{5,7},{6,0},{7,1},{8,10},{9,11},{10,... | collective-permute-start | bytes 1572872 | tf_op jit(solution)/shard_map/ppermute | solution.py:54
  9.2 13.9 %collective-permute-start.4 = (bf16[256,1024]{1,0:T(8,128)(2,1)S(1)}, bf16[256,1024]{1,0:T(8,128)(2,1)S(1)}, u32[]{:S(2)}, u32[]{:S(2)}) collective-permute-start(bf16[256,1024]{1,0:T(8,128)(2,1)S(1)} %convert_bitcast_fusion.refs_19_), channel_id=1, source_target_pairs={{0,6},{1,7},{2,0},{3,1},{4,2},{5,3},{6,4},{7,5},{8,14},{9,15},{10,... | collective-permute-start | bytes 1572872 | tf_op jit(solution)/shard_map/ppermute | solution.py:54
  12.5 11.9 %collective-permute-start.3 = (bf16[128,2048]{1,0:T(8,128)(2,1)S(1)}, bf16[128,2048]{1,0:T(8,128)(2,1)S(1)}, u32[]{:S(2)}, u32[]{:S(2)}) collective-permute-start(bf16[128,2048]{1,0:T(8,128)(2,1)S(1)} %pad_maximum_fusion.1), channel_id=1, source_target_pairs={{0,224},{8,40},{16,240},{24,56},{32,0},{40,72},{48,16},{56,88},{64... | collective-permute-start | bytes 1572872 | tf_op jit(solution)/shard_map/ppermute | solution.py:42
  13.9 14.5 %collective-permute-start.9 = (bf16[256,1024]{1,0:T(8,128)(2,1)S(1)}, bf16[256,1024]{1,0:T(8,128)(2,1)S(1)}, u32[]{:S(2)}, u32[]{:S(2)}) collective-permute-start(bf16[256,1024]{1,0:T(8,128)(2,1)S(1)} %convert_bitcast_fusion.refs_19_), channel_id=1, source_target_pairs={{0,1},{1,0},{2,3},{3,2},{4,5},{5,4},{6,7},{7,6},{8,9},{9,8},{10,11... | collective-permute-start | bytes 1572872 | tf_op jit(solution)/shard_map/ppermute | solution.py:50
  24.4 9.5 %collective-permute-start.6 = (bf16[128,2048]{1,0:T(8,128)(2,1)S(1)}, bf16[128,2048]{1,0:T(8,128)(2,1)S(1)}, u32[]{:S(2)}, u32[]{:S(2)}) collective-permute-start(bf16[128,2048]{1,0:T(8,128)(2,1)S(1)} %fusion.13.refs_8_), channel_id=1, source_target_pairs={{0,224},{8,40},{16,240},{24,56},{32,0},{40,72},{48,16},{56,88},{64... | collective-permute-start | bytes 1572872 | tf_op jit(solution)/shard_map/ppermute | solution.py:42
  24.5 6.5 %collective-permute-start.8 = (bf16[128,1024]{1,0:T(8,128)(2,1)S(1)}, bf16[128,1024]{1,0:T(8,128)(2,1)S(1)}, u32[]{:S(2)}, u32[]{:S(2)}) collective-permute-start(bf16[128,1024]{1,0:T(8,128)(2,1)S(1)} %slice.129), channel_id=1, source_target_pairs={{0,2},{1,3},{2,4},{3,5},{4,6},{5,7},{6,0},{7,1},{8,10},{9,11},{10,... | collective-permute-start | bytes 786440 | tf_op jit(solution)/shard_map/ppermute | solution.py:54
  25.8 5.6 %collective-permute-start.7 = (bf16[128,1024]{1,0:T(8,128)(2,1)S(1)}, bf16[128,1024]{1,0:T(8,128)(2,1)S(1)}, u32[]{:S(2)}, u32[]{:S(2)}) collective-permute-start(bf16[128,1024]{1,0:T(8,128)(2,1)S(1)} %slice.127), channel_id=1, source_target_pairs={{0,6},{1,7},{2,0},{3,1},{4,2},{5,3},{6,4},{7,5},{8,14},{9,15},{10,... | collective-permute-start | bytes 786440 | tf_op jit(solution)/shard_map/ppermute | solution.py:54
  28.4 16.8 %collective-permute-start.17 = (bf16[256,1024]{1,0:T(8,128)(2,1)S(1)}, bf16[256,1024]{1,0:T(8,128)(2,1)S(1)}, u32[]{:S(2)}, u32[]{:S(2)}) collective-permute-start(bf16[256,1024]{1,0:T(8,128)(2,1)S(1)} %collective-permute-done.9.refs_18_), channel_id=1, source_target_pairs={{0,2},{1,3},{2,4},{3,5},{4,6},{5,7},{6,0},{7,1},{8,10},{9,11},{10,... | collective-permute-start | bytes 1572872 | tf_op jit(solution)/shard_map/ppermute | solution.py:54
  33.9 10.5 %collective-permute-start.10 = (bf16[128,2048]{1,0:T(8,128)(2,1)S(1)}, bf16[128,2048]{1,0:T(8,128)(2,1)S(1)}, u32[]{:S(2)}, u32[]{:S(2)}) collective-permute-start(bf16[128,2048]{1,0:T(8,128)(2,1)S(1)} %fusion.10.refs_9_), channel_id=1, source_target_pairs={{0,224},{8,40},{16,240},{24,56},{32,0},{40,72},{48,16},{56,88},{64... | collective-permute-start | bytes 1572872 | tf_op jit(solution)/shard_map/ppermute | solution.py:42
  34.1 23.2 %collective-permute-start.13 = (bf16[256,2048]{1,0:T(8,128)(2,1)S(1)}, bf16[256,2048]{1,0:T(8,128)(2,1)S(1)}, u32[]{:S(2)}, u32[]{:S(2)}) collective-permute-start(bf16[256,2048]{1,0:T(8,128)(2,1)S(1)} %pad_maximum_fusion), channel_id=1, source_target_pairs={{0,8},{8,0},{16,24},{24,16},{32,40},{40,32},{48,56},{56,48},{64,72... | collective-permute-start | bytes 3145736 | tf_op jit(solution)/shard_map/ppermute | solution.py:30
  40.8 15.4 %collective-permute-start.15 = (bf16[256,1024]{1,0:T(8,128)(2,1)S(1)}, bf16[256,1024]{1,0:T(8,128)(2,1)S(1)}, u32[]{:S(2)}, u32[]{:S(2)}) collective-permute-start(bf16[256,1024]{1,0:T(8,128)(2,1)S(1)} %collective-permute-done.9.refs_18_), channel_id=1, source_target_pairs={{0,6},{1,7},{2,0},{3,1},{4,2},{5,3},{6,4},{7,5},{8,14},{9,15},{10,... | collective-permute-start | bytes 1572872 | tf_op jit(solution)/shard_map/ppermute | solution.py:54
  43.1 13.2 %collective-permute-start.16 = (bf16[256,1024]{1,0:T(8,128)(2,1)S(1)}, bf16[256,1024]{1,0:T(8,128)(2,1)S(1)}, u32[]{:S(2)}, u32[]{:S(2)}) collective-permute-start(bf16[256,1024]{1,0:T(8,128)(2,1)S(1)} %pad_maximum_fusion.2), channel_id=1, source_target_pairs={{0,1},{1,0},{2,3},{3,2},{4,5},{5,4},{6,7},{7,6},{8,9},{9,8},{10,11... | collective-permute-start | bytes 1572872 | tf_op jit(solution)/shard_map/ppermute | solution.py:50
  44.4 6.6 %collective-permute-start.11 = (bf16[64,2048]{1,0:T(8,128)(2,1)S(1)}, bf16[64,2048]{1,0:T(8,128)(2,1)S(1)}, u32[]{:S(2)}, u32[]{:S(2)}) collective-permute-start(bf16[64,2048]{1,0:T(8,128)(2,1)S(1)} %slice.132), channel_id=1, source_target_pairs={{0,224},{8,40},{16,240},{24,56},{32,0},{40,72},{48,16},{56,88},{64... | collective-permute-start | bytes 786440 | tf_op jit(solution)/shard_map/ppermute | solution.py:42
  45.2 12.2 %collective-permute-start.14 = (bf16[128,2048]{1,0:T(8,128)(2,1)S(1)}, bf16[128,2048]{1,0:T(8,128)(2,1)S(1)}, u32[]{:S(2)}, u32[]{:S(2)}) collective-permute-start(bf16[128,2048]{1,0:T(8,128)(2,1)S(1)} %collective-permute-done.10.refs_10_), channel_id=1, source_target_pairs={{0,8},{8,0},{16,24},{24,16},{32,40},{40,32},{48,56},{56,48},{64,72... | collective-permute-start | bytes 1572872 | tf_op jit(solution)/shard_map/ppermute | solution.py:30
  51.1 6.3 %collective-permute-start.12 = (bf16[64,2048]{1,0:T(8,128)(2,1)S(1)}, bf16[64,2048]{1,0:T(8,128)(2,1)S(1)}, u32[]{:S(2)}, u32[]{:S(2)}) collective-permute-start(bf16[64,2048]{1,0:T(8,128)(2,1)S(1)} %collective-permute-done.11.refs_7_), channel_id=1, source_target_pairs={{0,8},{8,0},{16,24},{24,16},{32,40},{40,32},{48,56},{56,48},{64,72... | collective-permute-start | bytes 786440 | tf_op jit(solution)/shard_map/ppermute | solution.py:30
  78.4 6.8 %collective-permute-start.18 = (bf16[448,2048]{1,0:T(8,128)(2,1)S(1)}, bf16[448,2048]{1,0:T(8,128)(2,1)S(1)}, u32[]{:S(2)}, u32[]{:S(2)}) collective-permute-start(bf16[448,2048]{1,0:T(8,128)(2,1)S(1)} %get-tuple-element.35), channel_id=1, source_target_pairs={{0,8},{8,0},{16,24},{24,16},{32,40},{40,32},{48,56},{56,48},{64,72... | collective-permute-start | bytes 5505032 | tf_op jit(solution)/shard_map/ppermute | solution.py:30
  82.4 21.6 %collective-permute-start.22 = (bf16[256,1024]{1,0:T(8,128)(2,1)S(1)}, bf16[256,1024]{1,0:T(8,128)(2,1)S(1)}, u32[]{:S(2)}, u32[]{:S(2)}) collective-permute-start(bf16[256,1024]{1,0:T(8,128)(2,1)S(1)} %get-tuple-element.45), channel_id=1, source_target_pairs={{0,6},{1,7},{2,0},{3,1},{4,2},{5,3},{6,4},{7,5},{8,14},{9,15},{10,... | collective-permute-start | bytes 1572872 | tf_op jit(solution)/shard_map/ppermute | solution.py:54
  83.6 17.3 %collective-permute-start.23 = (bf16[256,1024]{1,0:T(8,128)(2,1)S(1)}, bf16[256,1024]{1,0:T(8,128)(2,1)S(1)}, u32[]{:S(2)}, u32[]{:S(2)}) collective-permute-start(bf16[256,1024]{1,0:T(8,128)(2,1)S(1)} %get-tuple-element.47), channel_id=1, source_target_pairs={{0,1},{1,0},{2,3},{3,2},{4,5},{5,4},{6,7},{7,6},{8,9},{9,8},{10,11... | collective-permute-start | bytes 1572872 | tf_op jit(solution)/shard_map/ppermute | solution.py:50
  85.0 19.0 %collective-permute-start.21 = (bf16[256,1024]{1,0:T(8,128)(2,1)S(1)}, bf16[256,1024]{1,0:T(8,128)(2,1)S(1)}, u32[]{:S(2)}, u32[]{:S(2)}) collective-permute-start(bf16[256,1024]{1,0:T(8,128)(2,1)S(1)} %get-tuple-element.42), channel_id=1, source_target_pairs={{0,2},{1,3},{2,4},{3,5},{4,6},{5,7},{6,0},{7,1},{8,10},{9,11},{10,... | collective-permute-start | bytes 1572872 | tf_op jit(solution)/shard_map/ppermute | solution.py:54
  85.2 7.4 %collective-permute-start.19 = (bf16[64,2048]{1,0:T(8,128)(2,1)S(1)}, bf16[64,2048]{1,0:T(8,128)(2,1)S(1)}, u32[]{:S(2)}, u32[]{:S(2)}) collective-permute-start(bf16[64,2048]{1,0:T(8,128)(2,1)S(1)} %add_convert_fusion.8), channel_id=1, source_target_pairs={{0,32},{8,232},{16,48},{24,248},{32,64},{40,8},{48,80},{56,24},{64... | collective-permute-start | bytes 786440 | tf_op jit(solution)/shard_map/ppermute | solution.py:46
  92.8 11.9 %collective-permute-start.20 = (bf16[128,2048]{1,0:T(8,128)(2,1)S(1)}, bf16[128,2048]{1,0:T(8,128)(2,1)S(1)}, u32[]{:S(2)}, u32[]{:S(2)}) collective-permute-start(bf16[128,2048]{1,0:T(8,128)(2,1)S(1)} %add_convert_fusion.6), channel_id=1, source_target_pairs={{0,32},{8,232},{16,48},{24,248},{32,64},{40,8},{48,80},{56,24},{64... | collective-permute-start | bytes 1572872 | tf_op jit(solution)/shard_map/ppermute | solution.py:46
  101.2 12.1 %collective-permute-start.25 = (bf16[128,1024]{1,0:T(8,128)(2,1)S(1)}, bf16[128,1024]{1,0:T(8,128)(2,1)S(1)}, u32[]{:S(2)}, u32[]{:S(2)}) collective-permute-start(bf16[128,1024]{1,0:T(8,128)(2,1)S(1)} %get-tuple-element.56), channel_id=1, source_target_pairs={{0,2},{1,3},{2,4},{3,5},{4,6},{5,7},{6,0},{7,1},{8,10},{9,11},{10,... | collective-permute-start | bytes 786440 | tf_op jit(solution)/shard_map/ppermute | solution.py:54
  101.3 8.4 %collective-permute-start.26 = (bf16[128,1024]{1,0:T(8,128)(2,1)S(1)}, bf16[128,1024]{1,0:T(8,128)(2,1)S(1)}, u32[]{:S(2)}, u32[]{:S(2)}) collective-permute-start(bf16[128,1024]{1,0:T(8,128)(2,1)S(1)} %get-tuple-element.57), channel_id=1, source_target_pairs={{0,6},{1,7},{2,0},{3,1},{4,2},{5,3},{6,4},{7,5},{8,14},{9,15},{10,... | collective-permute-start | bytes 786440 | tf_op jit(solution)/shard_map/ppermute | solution.py:54
  104.3 13.8 %collective-permute-start.30 = (bf16[256,1024]{1,0:T(8,128)(2,1)S(1)}, bf16[256,1024]{1,0:T(8,128)(2,1)S(1)}, u32[]{:S(2)}, u32[]{:S(2)}) collective-permute-start(bf16[256,1024]{1,0:T(8,128)(2,1)S(1)} %add_convert_fusion.5), channel_id=1, source_target_pairs={{0,1},{1,0},{2,3},{3,2},{4,5},{5,4},{6,7},{7,6},{8,9},{9,8},{10,11... | collective-permute-start | bytes 1572872 | tf_op jit(solution)/shard_map/ppermute | solution.py:50
  104.9 8.5 %collective-permute-start.24 = (bf16[128,2048]{1,0:T(8,128)(2,1)S(1)}, bf16[128,2048]{1,0:T(8,128)(2,1)S(1)}, u32[]{:S(2)}, u32[]{:S(2)}) collective-permute-start(bf16[128,2048]{1,0:T(8,128)(2,1)S(1)} %add_convert_fusion.3), channel_id=1, source_target_pairs={{0,32},{8,232},{16,48},{24,248},{32,64},{40,8},{48,80},{56,24},{64... | collective-permute-start | bytes 1572872 | tf_op jit(solution)/shard_map/ppermute | solution.py:46
  109.8 14.9 %collective-permute-start.29 = (bf16[256,1024]{1,0:T(8,128)(2,1)S(1)}, bf16[256,1024]{1,0:T(8,128)(2,1)S(1)}, u32[]{:S(2)}, u32[]{:S(2)}) collective-permute-start(bf16[256,1024]{1,0:T(8,128)(2,1)S(1)} %add_convert_fusion.1), channel_id=1, source_target_pairs={{0,6},{1,7},{2,0},{3,1},{4,2},{5,3},{6,4},{7,5},{8,14},{9,15},{10,... | collective-permute-start | bytes 1572872 | tf_op jit(solution)/shard_map/ppermute | solution.py:54
  113.3 14.5 %collective-permute-start.28 = (bf16[256,1024]{1,0:T(8,128)(2,1)S(1)}, bf16[256,1024]{1,0:T(8,128)(2,1)S(1)}, u32[]{:S(2)}, u32[]{:S(2)}) collective-permute-start(bf16[256,1024]{1,0:T(8,128)(2,1)S(1)} %add_convert_fusion.2), channel_id=1, source_target_pairs={{0,2},{1,3},{2,4},{3,5},{4,6},{5,7},{6,0},{7,1},{8,10},{9,11},{10,... | collective-permute-start | bytes 1572872 | tf_op jit(solution)/shard_map/ppermute | solution.py:54
  113.7 14.2 %collective-permute-start.27 = (bf16[128,2048]{1,0:T(8,128)(2,1)S(1)}, bf16[128,2048]{1,0:T(8,128)(2,1)S(1)}, u32[]{:S(2)}, u32[]{:S(2)}) collective-permute-start(bf16[128,2048]{1,0:T(8,128)(2,1)S(1)} %add_convert_fusion), channel_id=1, source_target_pairs={{0,32},{8,232},{16,48},{24,248},{32,64},{40,8},{48,80},{56,24},{64... | collective-permute-start | bytes 1572872 | tf_op jit(solution)/shard_map/ppermute | solution.py:46
  130.4 6.3 %collective-permute-start.32 = (bf16[32,2048]{1,0:T(8,128)(2,1)S(1)}, bf16[32,2048]{1,0:T(8,128)(2,1)S(1)}, u32[]{:S(2)}, u32[]{:S(2)}) collective-permute-start(bf16[32,2048]{1,0:T(8,128)(2,1)S(1)} %slice.206), channel_id=1, source_target_pairs={{0,16},{8,24},{16,0},{24,8},{32,48},{40,56},{48,32},{56,40},{64,80... | collective-permute-start | bytes 393224 | tf_op jit(solution)/shard_map/ppermute | solution.py:34
  (7 other events, 98.1 us)
where the time goes:
time: 138 us
  starting transfers between devices  57.9 us (42%)
  waiting for transfers between devices  36.5 us (26%)
  Pallas kernels  35.3 us (26%)
  other arithmetic  6.76 us (5%)
    ppermute x12, waiting for transfers between devices, from_x(): return lax.ppermute(a, 'col', [(i, (i - 2 * k) % 8) for i in range(8)])  24.6 us
    ppermute x6, starting transfers between devices, swap_core(): return lax.ppermute(a, 'row', [(i, i ^ 1) for i in range(32)])  19.3 us
    pallas_call x1, Pallas kernels, inner_steps(): pl.pallas_call(kernel, out_shape=(jax.ShapeDtypeStruct((2, TOK, FFW), bf1...  16.7 us
    ppermute x12, starting transfers between devices, from_x(): return lax.ppermute(a, 'col', [(i, (i - 2 * k) % 8) for i in range(8)])  15.7 us
    pallas_call x2, Pallas kernels, down_change(): pl.pallas_call(kernel, grid=(D // BLK,), out_shape=(jax.ShapeDtypeStruct(...  9 us
    pallas_call x2, Pallas kernels, up_change(): pl.pallas_call(kernel, grid=(FFW // wide,), out_shape=tuple((jax.ShapeDty...  8.51 us
    ppermute x4, starting transfers between devices, to_z(): lax.ppermute(a, 'row', [(i, (i + (-4 if i % 2 else 4)) % 32) for i in ran...  6.9 us
    ppermute x4, starting transfers between devices, swap_yl(): return lax.ppermute(a, 'col', [(i, i ^ 1) for i in range(8)])  4.81 us
  transfers between devices with their start and end apart: 33, of which 14 were waited for; matrix products, arithmetic and copies ran while one was open for 4% of the time, Pallas kernels for 10%

commit v1 on v0

--- a/solution.py
+++ b/solution.py
@@ -271,7 +271,7 @@
     grad_out(0, sd)
     grad_pre(0, sd)
 
-    @pl.loop(0, 8, unroll=2)
+    @pl.loop(0, 8, unroll=4)
     def _(k):
         raw = dot(nt_ref[0], gp_ref[0, :, columns(k)])
         w1u[...] = first_weight(su[:, columns(k)], raw, width_scale).astype(bf16)

time: 138 us -> 138 us (level)
  no operation moved by 1% of the time
where the time goes in v1:
time: 138 us
  starting transfers between devices  57.9 us (42%)
  waiting for transfers between devices  36.6 us (27%)
  Pallas kernels  35.3 us (26%)
  other arithmetic  6.76 us (5%)
    ppermute x12, waiting for transfers between devices, from_x(): return lax.ppermute(a, 'col', [(i, (i - 2 * k) % 8) for i in range(8)])  24.6 us
    ppermute x6, starting transfers between devices, swap_core(): return lax.ppermute(a, 'row', [(i, i ^ 1) for i in range(32)])  19.3 us
    pallas_call x1, Pallas kernels, inner_steps(): pl.pallas_call(kernel, out_shape=(jax.ShapeDtypeStruct((2, TOK, FFW), bf1...  16.8 us
    ppermute x12, starting transfers between devices, from_x(): return lax.ppermute(a, 'col', [(i, (i - 2 * k) % 8) for i in range(8)])  15.7 us
    pallas_call x2, Pallas kernels, down_change(): pl.pallas_call(kernel, grid=(D // BLK,), out_shape=(jax.ShapeDtypeStruct(...  9 us
    pallas_call x2, Pallas kernels, up_change(): pl.pallas_call(kernel, grid=(FFW // wide,), out_shape=tuple((jax.ShapeDty...  8.51 us
    ppermute x4, starting transfers between devices, to_z(): lax.ppermute(a, 'row', [(i, (i + (-4 if i % 2 else 4)) % 32) for i in ran...  6.94 us
    ppermute x4, starting transfers between devices, swap_yl(): return lax.ppermute(a, 'col', [(i, i ^ 1) for i in range(8)])  4.8 us
  transfers between devices with their start and end apart: 33, of which 14 were waited for; matrix products, arithmetic and copies ran while one was open for 4% of the time, Pallas kernels for 10%

profile of v1, /device:TPU:1, one launch (start us, length us, event | category | flops | bytes accessed | tf_op | source)
XLA Modules:
  0.0 137.6 jit_solution(2403326437956817841)
XLA Ops:
  1.6 4.4 %collective-permute-start.2 = (bf16[32,2048]{1,0:T(8,128)(2,1)S(1)}, bf16[32,2048]{1,0:T(8,128)(2,1)S(1)}, u32[]{:S(2)}, u32[]{:S(2)}) collective-permute-start(bf16[32,2048]{1,0:T(8,128)(2,1)S(1)} %convert_bitcast_fusion.1.refs_11_), channel_id=1, source_target_pairs={{0,24},{8,16},{16,8},{24,0},{32,56},{40,48},{48,40},{56,32},{64,88... | collective-permute-start | bytes 393224 | tf_op jit(solution)/shard_map/ppermute | solution.py:38
  6.0 1.8 %collective-permute-start = (bf16[32,2048]{1,0:T(8,128)(2,1)S(1)}, bf16[32,2048]{1,0:T(8,128)(2,1)S(1)}, u32[]{:S(2)}, u32[]{:S(2)}) collective-permute-start(bf16[32,2048]{1,0:T(8,128)(2,1)S(1)} %convert_bitcast_fusion.1.refs_11_), channel_id=1, source_target_pairs={{0,16},{8,24},{16,0},{24,8},{32,48},{40,56},{48,32},{56,40},{64,80... | collective-permute-start | bytes 393224 | tf_op jit(solution)/shard_map/ppermute | solution.py:34
  7.8 1.3 convert_bitcast_fusion.refs_19_
  9.2 2.7 %collective-permute-start.4 = (bf16[256,1024]{1,0:T(8,128)(2,1)S(1)}, bf16[256,1024]{1,0:T(8,128)(2,1)S(1)}, u32[]{:S(2)}, u32[]{:S(2)}) collective-permute-start(bf16[256,1024]{1,0:T(8,128)(2,1)S(1)} %convert_bitcast_fusion.refs_19_), channel_id=1, source_target_pairs={{0,6},{1,7},{2,0},{3,1},{4,2},{5,3},{6,4},{7,5},{8,14},{9,15},{10,... | collective-permute-start | bytes 1572872 | tf_op jit(solution)/shard_map/ppermute | solution.py:54
  12.5 1.4 %collective-permute-start.3 = (bf16[128,2048]{1,0:T(8,128)(2,1)S(1)}, bf16[128,2048]{1,0:T(8,128)(2,1)S(1)}, u32[]{:S(2)}, u32[]{:S(2)}) collective-permute-start(bf16[128,2048]{1,0:T(8,128)(2,1)S(1)} %pad_maximum_fusion.1), channel_id=1, source_target_pairs={{0,224},{8,40},{16,240},{24,56},{32,0},{40,72},{48,16},{56,88},{64... | collective-permute-start | bytes 1572872 | tf_op jit(solution)/shard_map/ppermute | solution.py:42
  13.9 1.9 %collective-permute-start.9 = (bf16[256,1024]{1,0:T(8,128)(2,1)S(1)}, bf16[256,1024]{1,0:T(8,128)(2,1)S(1)}, u32[]{:S(2)}, u32[]{:S(2)}) collective-permute-start(bf16[256,1024]{1,0:T(8,128)(2,1)S(1)} %convert_bitcast_fusion.refs_19_), channel_id=1, source_target_pairs={{0,1},{1,0},{2,3},{3,2},{4,5},{5,4},{6,7},{7,6},{8,9},{9,8},{10,11... | collective-permute-start | bytes 1572872 | tf_op jit(solution)/shard_map/ppermute | solution.py:50
  15.7 7.3 %collective-permute-done.5.refs_23_ = bf16[256,1024]{1,0:T(8,128)(2,1)S(1)} collective-permute-done((bf16[256,1024]{1,0:T(8,128)(2,1)S(1)}, bf16[256,1024]{1,0:T(8,128)(2,1)S(1)}, u32[]{:S(2)}, u32[]{:S(2)}) %collective-permute-start.5) | collective-permute-done | bytes 524320 | tf_op jit(solution)/shard_map/ppermute | solution.py:54
  23.1 1.3 collective-permute-done.3
  25.8 1.5 %collective-permute-start.7 = (bf16[128,1024]{1,0:T(8,128)(2,1)S(1)}, bf16[128,1024]{1,0:T(8,128)(2,1)S(1)}, u32[]{:S(2)}, u32[]{:S(2)}) collective-permute-start(bf16[128,1024]{1,0:T(8,128)(2,1)S(1)} %slice.127), channel_id=1, source_target_pairs={{0,6},{1,7},{2,0},{3,1},{4,2},{5,3},{6,4},{7,5},{8,14},{9,15},{10,... | collective-permute-start | bytes 786440 | tf_op jit(solution)/shard_map/ppermute | solution.py:54
  28.5 2.5 %collective-permute-done.8.refs_22_ = bf16[128,1024]{1,0:T(8,128)(2,1)S(1)} collective-permute-done((bf16[128,1024]{1,0:T(8,128)(2,1)S(1)}, bf16[128,1024]{1,0:T(8,128)(2,1)S(1)}, u32[]{:S(2)}, u32[]{:S(2)}) %collective-permute-start.8) | collective-permute-done | bytes 262176 | tf_op jit(solution)/shard_map/ppermute | solution.py:54
  31.4 2.5 %collective-permute-done.6 = bf16[128,2048]{1,0:T(8,128)(2,1)S(1)} collective-permute-done((bf16[128,2048]{1,0:T(8,128)(2,1)S(1)}, bf16[128,2048]{1,0:T(8,128)(2,1)S(1)}, u32[]{:S(2)}, u32[]{:S(2)}) %collective-permute-start.6) | collective-permute-done | bytes 524320 | tf_op jit(solution)/shard_map/ppermute | solution.py:42
  34.1 6.6 %collective-permute-start.13 = (bf16[256,2048]{1,0:T(8,128)(2,1)S(1)}, bf16[256,2048]{1,0:T(8,128)(2,1)S(1)}, u32[]{:S(2)}, u32[]{:S(2)}) collective-permute-start(bf16[256,2048]{1,0:T(8,128)(2,1)S(1)} %pad_maximum_fusion), channel_id=1, source_target_pairs={{0,8},{8,0},{16,24},{24,16},{32,40},{40,32},{48,56},{56,48},{64,72... | collective-permute-start | bytes 3145736 | tf_op jit(solution)/shard_map/ppermute | solution.py:30
  40.8 2.3 %collective-permute-start.15 = (bf16[256,1024]{1,0:T(8,128)(2,1)S(1)}, bf16[256,1024]{1,0:T(8,128)(2,1)S(1)}, u32[]{:S(2)}, u32[]{:S(2)}) collective-permute-start(bf16[256,1024]{1,0:T(8,128)(2,1)S(1)} %collective-permute-done.9.refs_18_), channel_id=1, source_target_pairs={{0,6},{1,7},{2,0},{3,1},{4,2},{5,3},{6,4},{7,5},{8,14},{9,15},{10,... | collective-permute-start | bytes 1572872 | tf_op jit(solution)/shard_map/ppermute | solution.py:54
  45.2 5.9 %collective-permute-start.14 = (bf16[128,2048]{1,0:T(8,128)(2,1)S(1)}, bf16[128,2048]{1,0:T(8,128)(2,1)S(1)}, u32[]{:S(2)}, u32[]{:S(2)}) collective-permute-start(bf16[128,2048]{1,0:T(8,128)(2,1)S(1)} %collective-permute-done.10.refs_10_), channel_id=1, source_target_pairs={{0,8},{8,0},{16,24},{24,16},{32,40},{40,32},{48,56},{56,48},{64,72... | collective-permute-start | bytes 1572872 | tf_op jit(solution)/shard_map/ppermute | solution.py:30
  51.1 5.1 %collective-permute-start.12 = (bf16[64,2048]{1,0:T(8,128)(2,1)S(1)}, bf16[64,2048]{1,0:T(8,128)(2,1)S(1)}, u32[]{:S(2)}, u32[]{:S(2)}) collective-permute-start(bf16[64,2048]{1,0:T(8,128)(2,1)S(1)} %collective-permute-done.11.refs_7_), channel_id=1, source_target_pairs={{0,8},{8,0},{16,24},{24,16},{32,40},{40,32},{48,56},{56,48},{64,72... | collective-permute-start | bytes 786440 | tf_op jit(solution)/shard_map/ppermute | solution.py:30
  57.4 16.8 %inner_steps.1 = (bf16[2,128,2048]{2,1,0:T(8,128)(2,1)S(1)}, bf16[2,128,1024]{2,1,0:T(8,128)(2,1)S(1)}, bf16[2,128,2048]{2,1,0:T(8,128)(2,1)S(1)}, bf16[512,2048...) custom-call(bf16[2,128,1024]{2,1,0:T(8,128)(2,1)S(1)} %get-tuple-ele, ...), custom_call_target="tpu_custom_call" | custom-call | flops 5000000000 | bytes 25165824 | tf_op jit(solution)/shard_map/inner_steps/pallas_call | solution.py:298
  74.2 4.2 %up_change.3 = (bf16[448,2048]{1,0:T(8,128)(2,1)S(1)}, bf16[64,2048]{1,0:T(8,128)(2,1)S(1)}) custom-call(bf16[512,2048]{1,0:T(8,128)(2,1)S(1)} %get-tuple-element.34.s_ref, bf16[2,1024,128]{2,1,0:T(8,128)(2,1)S(1)} %get-tuple-element.29.refs_1_.n_ref, bf16[2,128,2048]{2,1,0:T(8,128)(2,1)S(1)} %get-tuple-element.31.g_ref), custom_call_target="tpu_custom_call" | custom-call | flops 536870912 | bytes 4194304 | tf_op jit(solution)/shard_map/up_change/pallas_call | solution.py:340
  78.9 3.6 %down_change.2 = (bf16[256,1024]{1,0:T(8,128)(2,1)S(1)}, bf16[256,1024]{1,0:T(8,128)(2,1)S(1)}, bf16[256,1024]{1,0:T(8,128)(2,1)S(1)}) custom-call(bf16[768,1024]{1,0:T(8,128)(2,1)S(1)} %get-tuple-element.39.s_ref, bf16[2,128,2048]{2,1,0:T(8,128)(2,1)S(1)} %get-tuple-element.40.a_ref, bf16[2,128,1024]{2,1,0:T(8,128)(2,1)S(1)} %get-tuple-element.41.g_ref), custom_call_target="tpu_custom_call" | custom-call | flops 402653184 | bytes 3145728 | tf_op jit(solution)/shard_map/down_change/pallas_call | solution.py:367
  83.7 1.3 collective-permute-start.23
  85.3 3.3 %collective-permute-start.19 = (bf16[64,2048]{1,0:T(8,128)(2,1)S(1)}, bf16[64,2048]{1,0:T(8,128)(2,1)S(1)}, u32[]{:S(2)}, u32[]{:S(2)}) collective-permute-start(bf16[64,2048]{1,0:T(8,128)(2,1)S(1)} %add_convert_fusion.8), channel_id=1, source_target_pairs={{0,32},{8,232},{16,48},{24,248},{32,64},{40,8},{48,80},{56,24},{64... | collective-permute-start | bytes 786440 | tf_op jit(solution)/shard_map/ppermute | solution.py:46
  88.6 4.3 %up_change.2 = (bf16[128,2048]{1,0:T(8,128)(2,1)S(1)}, bf16[128,2048]{1,0:T(8,128)(2,1)S(1)}, bf16[128,2048]{1,0:T(8,128)(2,1)S(1)}, bf16[64,2048]{1,0:T(8,128)(2,1)S(1)}, bf16[64,2048]{1,0:T(8,128)(2,1)S(1)}) custom-call(bf16[512,2048]{1,0:T(8,128)(2,1)S(1)} %get-tuple-element.30.s_ref, bf16[2,1024,128]{2,1,0:T(8,128)(2,1)S(1)} %get-tuple-element.29.refs_1_.n_ref, ...), custom_call_target="tpu_custom_call" | custom-call | flops 536870912 | bytes 4194304 | tf_op jit(solution)/shard_map/up_change/pallas_call | solution.py:340
  93.1 2.5 %collective-permute-start.20 = (bf16[128,2048]{1,0:T(8,128)(2,1)S(1)}, bf16[128,2048]{1,0:T(8,128)(2,1)S(1)}, u32[]{:S(2)}, u32[]{:S(2)}) collective-permute-start(bf16[128,2048]{1,0:T(8,128)(2,1)S(1)} %add_convert_fusion.6), channel_id=1, source_target_pairs={{0,32},{8,232},{16,48},{24,248},{32,64},{40,8},{48,80},{56,24},{64... | collective-permute-start | bytes 1572872 | tf_op jit(solution)/shard_map/ppermute | solution.py:46
  95.6 5.4 %down_change.3 = (bf16[256,1024]{1,0:T(8,128)(2,1)S(1)}, bf16[256,1024]{1,0:T(8,128)(2,1)S(1)}, bf16[256,1024]{1,0:T(8,128)(2,1)S(1)}, bf16[256,1024]{1,0:T(8,128)(2,1)S(1)}, bf16[256,1024]{1,0:T(8,128)(2,1)S(1)}) custom-call(bf16[1280,1024]{1,0:T(8,128)(2,1)S(1)} %get-tuple-element.43.s_ref, bf16[2,128,2048]{2,1,0:T(8,128)(2,1)S(1)} %get-tuple-element.40.a_ref, ...), custom_call_target="tpu_custom_call" | custom-call | flops 671088640 | bytes 5242880 | tf_op jit(solution)/shard_map/down_change/pallas_call | solution.py:367
  101.3 2.8 %collective-permute-start.26 = (bf16[128,1024]{1,0:T(8,128)(2,1)S(1)}, bf16[128,1024]{1,0:T(8,128)(2,1)S(1)}, u32[]{:S(2)}, u32[]{:S(2)}) collective-permute-start(bf16[128,1024]{1,0:T(8,128)(2,1)S(1)} %get-tuple-element.57), channel_id=1, source_target_pairs={{0,6},{1,7},{2,0},{3,1},{4,2},{5,3},{6,4},{7,5},{8,14},{9,15},{10,... | collective-permute-start | bytes 786440 | tf_op jit(solution)/shard_map/ppermute | solution.py:54
  105.1 4.6 %collective-permute-done.26 = bf16[128,1024]{1,0:T(8,128)(2,1)S(1)} collective-permute-done((bf16[128,1024]{1,0:T(8,128)(2,1)S(1)}, bf16[128,1024]{1,0:T(8,128)(2,1)S(1)}, u32[]{:S(2)}, u32[]{:S(2)}) %collective-permute-start.26) | collective-permute-done | bytes 262176 | tf_op jit(solution)/shard_map/ppermute | solution.py:54
  109.8 3.5 %collective-permute-start.29 = (bf16[256,1024]{1,0:T(8,128)(2,1)S(1)}, bf16[256,1024]{1,0:T(8,128)(2,1)S(1)}, u32[]{:S(2)}, u32[]{:S(2)}) collective-permute-start(bf16[256,1024]{1,0:T(8,128)(2,1)S(1)} %add_convert_fusion.1), channel_id=1, source_target_pairs={{0,6},{1,7},{2,0},{3,1},{4,2},{5,3},{6,4},{7,5},{8,14},{9,15},{10,... | collective-permute-start | bytes 1572872 | tf_op jit(solution)/shard_map/ppermute | solution.py:54
  114.7 3.5 %collective-permute-done.30 = bf16[256,1024]{1,0:T(8,128)(2,1)S(1)} collective-permute-done((bf16[256,1024]{1,0:T(8,128)(2,1)S(1)}, bf16[256,1024]{1,0:T(8,128)(2,1)S(1)}, u32[]{:S(2)}, u32[]{:S(2)}) %collective-permute-start.30) | collective-permute-done | bytes 524320 | tf_op jit(solution)/shard_map/ppermute | solution.py:50
  118.2 6.5 %collective-permute-done.29 = bf16[256,1024]{1,0:T(8,128)(2,1)S(1)} collective-permute-done((bf16[256,1024]{1,0:T(8,128)(2,1)S(1)}, bf16[256,1024]{1,0:T(8,128)(2,1)S(1)}, u32[]{:S(2)}, u32[]{:S(2)}) %collective-permute-start.29) | collective-permute-done | bytes 524320 | tf_op jit(solution)/shard_map/ppermute | solution.py:54
  124.7 3.3 %collective-permute-done.28 = bf16[256,1024]{1,0:T(8,128)(2,1)S(1)} collective-permute-done((bf16[256,1024]{1,0:T(8,128)(2,1)S(1)}, bf16[256,1024]{1,0:T(8,128)(2,1)S(1)}, u32[]{:S(2)}, u32[]{:S(2)}) %collective-permute-start.28) | collective-permute-done | bytes 524320 | tf_op jit(solution)/shard_map/ppermute | solution.py:54
  130.5 2.7 %collective-permute-start.32 = (bf16[32,2048]{1,0:T(8,128)(2,1)S(1)}, bf16[32,2048]{1,0:T(8,128)(2,1)S(1)}, u32[]{:S(2)}, u32[]{:S(2)}) collective-permute-start(bf16[32,2048]{1,0:T(8,128)(2,1)S(1)} %slice.206), channel_id=1, source_target_pairs={{0,16},{8,24},{16,0},{24,8},{32,48},{40,56},{48,32},{56,40},{64,80... | collective-permute-start | bytes 393224 | tf_op jit(solution)/shard_map/ppermute | solution.py:34
  133.2 1.9 %fusion.1 = (f32[1,256,1024]{2,1,0:T(8,128)}, f32[1,256,1024]{2,1,0:T(8,128)}) fusion(f32[1,256,1024]{2,1,0:T(8,128)S(1)} %copy-done.2, bf16[256,1024]{1,0:T(8,128)(2,1)S(1)} %collective-permute-done.29, bf16[256,1024]{1,0:T(8,128)(2,1)S(1)} %collective-permute-done.28, bf16[256,1024]{1,0:T(8,128)(2,1)S(1)} %collective-permute-done.30, ...), kind=kLoop, calls=%fused_computation.4 | loop fusion | flops 3670016 | bytes 6291456 | tf_op jit(solution)/shard_map/sub | solution.py:412
  135.1 1.7 %collective-permute-done.32 = bf16[32,2048]{1,0:T(8,128)(2,1)S(1)} collective-permute-done((bf16[32,2048]{1,0:T(8,128)(2,1)S(1)}, bf16[32,2048]{1,0:T(8,128)(2,1)S(1)}, u32[]{:S(2)}, u32[]{:S(2)}) %collective-permute-start.32) | collective-permute-done | bytes 131104 | tf_op jit(solution)/shard_map/ppermute | solution.py:34
  (80 shorter events, 16.3 us)
Async XLA Ops:
  1.6 10.2 %collective-permute-start.2 = (bf16[32,2048]{1,0:T(8,128)(2,1)S(1)}, bf16[32,2048]{1,0:T(8,128)(2,1)S(1)}, u32[]{:S(2)}, u32[]{:S(2)}) collective-permute-start(bf16[32,2048]{1,0:T(8,128)(2,1)S(1)} %convert_bitcast_fusion.1.refs_11_), channel_id=1, source_target_pairs={{0,24},{8,16},{16,8},{24,0},{32,56},{40,48},{48,40},{56,32},{64,88... | collective-permute-start | bytes 393224 | tf_op jit(solution)/shard_map/ppermute | solution.py:38
  6.0 5.9 %collective-permute-start.1 = (bf16[32,2048]{1,0:T(8,128)(2,1)S(1)}, bf16[32,2048]{1,0:T(8,128)(2,1)S(1)}, u32[]{:S(2)}, u32[]{:S(2)}) collective-permute-start(bf16[32,2048]{1,0:T(8,128)(2,1)S(1)} %convert_bitcast_fusion.1.refs_11_), channel_id=1, source_target_pairs={{0,8},{8,0},{16,24},{24,16},{32,40},{40,32},{48,56},{56,48},{64,72... | collective-permute-start | bytes 393224 | tf_op jit(solution)/shard_map/ppermute | solution.py:30
  6.0 6.4 %collective-permute-start = (bf16[32,2048]{1,0:T(8,128)(2,1)S(1)}, bf16[32,2048]{1,0:T(8,128)(2,1)S(1)}, u32[]{:S(2)}, u32[]{:S(2)}) collective-permute-start(bf16[32,2048]{1,0:T(8,128)(2,1)S(1)} %convert_bitcast_fusion.1.refs_11_), channel_id=1, source_target_pairs={{0,16},{8,24},{16,0},{24,8},{32,48},{40,56},{48,32},{56,40},{64,80... | collective-permute-start | bytes 393224 | tf_op jit(solution)/shard_map/ppermute | solution.py:34
  9.1 13.9 %collective-permute-start.5 = (bf16[256,1024]{1,0:T(8,128)(2,1)S(1)}, bf16[256,1024]{1,0:T(8,128)(2,1)S(1)}, u32[]{:S(2)}, u32[]{:S(2)}) collective-permute-start(bf16[256,1024]{1,0:T(8,128)(2,1)S(1)} %convert_bitcast_fusion.refs_19_), channel_id=1, source_target_pairs={{0,2},{1,3},{2,4},{3,5},{4,6},{5,7},{6,0},{7,1},{8,10},{9,11},{10,... | collective-permute-start | bytes 1572872 | tf_op jit(solution)/shard_map/ppermute | solution.py:54
  9.2 13.9 %collective-permute-start.4 = (bf16[256,1024]{1,0:T(8,128)(2,1)S(1)}, bf16[256,1024]{1,0:T(8,128)(2,1)S(1)}, u32[]{:S(2)}, u32[]{:S(2)}) collective-permute-start(bf16[256,1024]{1,0:T(8,128)(2,1)S(1)} %convert_bitcast_fusion.refs_19_), channel_id=1, source_target_pairs={{0,6},{1,7},{2,0},{3,1},{4,2},{5,3},{6,4},{7,5},{8,14},{9,15},{10,... | collective-permute-start | bytes 1572872 | tf_op jit(solution)/shard_map/ppermute | solution.py:54
  12.5 11.9 %collective-permute-start.3 = (bf16[128,2048]{1,0:T(8,128)(2,1)S(1)}, bf16[128,2048]{1,0:T(8,128)(2,1)S(1)}, u32[]{:S(2)}, u32[]{:S(2)}) collective-permute-start(bf16[128,2048]{1,0:T(8,128)(2,1)S(1)} %pad_maximum_fusion.1), channel_id=1, source_target_pairs={{0,224},{8,40},{16,240},{24,56},{32,0},{40,72},{48,16},{56,88},{64... | collective-permute-start | bytes 1572872 | tf_op jit(solution)/shard_map/ppermute | solution.py:42
  13.9 14.5 %collective-permute-start.9 = (bf16[256,1024]{1,0:T(8,128)(2,1)S(1)}, bf16[256,1024]{1,0:T(8,128)(2,1)S(1)}, u32[]{:S(2)}, u32[]{:S(2)}) collective-permute-start(bf16[256,1024]{1,0:T(8,128)(2,1)S(1)} %convert_bitcast_fusion.refs_19_), channel_id=1, source_target_pairs={{0,1},{1,0},{2,3},{3,2},{4,5},{5,4},{6,7},{7,6},{8,9},{9,8},{10,11... | collective-permute-start | bytes 1572872 | tf_op jit(solution)/shard_map/ppermute | solution.py:50
  24.4 9.5 %collective-permute-start.6 = (bf16[128,2048]{1,0:T(8,128)(2,1)S(1)}, bf16[128,2048]{1,0:T(8,128)(2,1)S(1)}, u32[]{:S(2)}, u32[]{:S(2)}) collective-permute-start(bf16[128,2048]{1,0:T(8,128)(2,1)S(1)} %fusion.13.refs_8_), channel_id=1, source_target_pairs={{0,224},{8,40},{16,240},{24,56},{32,0},{40,72},{48,16},{56,88},{64... | collective-permute-start | bytes 1572872 | tf_op jit(solution)/shard_map/ppermute | solution.py:42
  24.5 6.5 %collective-permute-start.8 = (bf16[128,1024]{1,0:T(8,128)(2,1)S(1)}, bf16[128,1024]{1,0:T(8,128)(2,1)S(1)}, u32[]{:S(2)}, u32[]{:S(2)}) collective-permute-start(bf16[128,1024]{1,0:T(8,128)(2,1)S(1)} %slice.129), channel_id=1, source_target_pairs={{0,2},{1,3},{2,4},{3,5},{4,6},{5,7},{6,0},{7,1},{8,10},{9,11},{10,... | collective-permute-start | bytes 786440 | tf_op jit(solution)/shard_map/ppermute | solution.py:54
  25.8 5.6 %collective-permute-start.7 = (bf16[128,1024]{1,0:T(8,128)(2,1)S(1)}, bf16[128,1024]{1,0:T(8,128)(2,1)S(1)}, u32[]{:S(2)}, u32[]{:S(2)}) collective-permute-start(bf16[128,1024]{1,0:T(8,128)(2,1)S(1)} %slice.127), channel_id=1, source_target_pairs={{0,6},{1,7},{2,0},{3,1},{4,2},{5,3},{6,4},{7,5},{8,14},{9,15},{10,... | collective-permute-start | bytes 786440 | tf_op jit(solution)/shard_map/ppermute | solution.py:54
  28.4 16.8 %collective-permute-start.17 = (bf16[256,1024]{1,0:T(8,128)(2,1)S(1)}, bf16[256,1024]{1,0:T(8,128)(2,1)S(1)}, u32[]{:S(2)}, u32[]{:S(2)}) collective-permute-start(bf16[256,1024]{1,0:T(8,128)(2,1)S(1)} %collective-permute-done.9.refs_18_), channel_id=1, source_target_pairs={{0,2},{1,3},{2,4},{3,5},{4,6},{5,7},{6,0},{7,1},{8,10},{9,11},{10,... | collective-permute-start | bytes 1572872 | tf_op jit(solution)/shard_map/ppermute | solution.py:54
  33.9 10.5 %collective-permute-start.10 = (bf16[128,2048]{1,0:T(8,128)(2,1)S(1)}, bf16[128,2048]{1,0:T(8,128)(2,1)S(1)}, u32[]{:S(2)}, u32[]{:S(2)}) collective-permute-start(bf16[128,2048]{1,0:T(8,128)(2,1)S(1)} %fusion.10.refs_9_), channel_id=1, source_target_pairs={{0,224},{8,40},{16,240},{24,56},{32,0},{40,72},{48,16},{56,88},{64... | collective-permute-start | bytes 1572872 | tf_op jit(solution)/shard_map/ppermute | solution.py:42
  34.1 23.2 %collective-permute-start.13 = (bf16[256,2048]{1,0:T(8,128)(2,1)S(1)}, bf16[256,2048]{1,0:T(8,128)(2,1)S(1)}, u32[]{:S(2)}, u32[]{:S(2)}) collective-permute-start(bf16[256,2048]{1,0:T(8,128)(2,1)S(1)} %pad_maximum_fusion), channel_id=1, source_target_pairs={{0,8},{8,0},{16,24},{24,16},{32,40},{40,32},{48,56},{56,48},{64,72... | collective-permute-start | bytes 3145736 | tf_op jit(solution)/shard_map/ppermute | solution.py:30
  40.8 15.4 %collective-permute-start.15 = (bf16[256,1024]{1,0:T(8,128)(2,1)S(1)}, bf16[256,1024]{1,0:T(8,128)(2,1)S(1)}, u32[]{:S(2)}, u32[]{:S(2)}) collective-permute-start(bf16[256,1024]{1,0:T(8,128)(2,1)S(1)} %collective-permute-done.9.refs_18_), channel_id=1, source_target_pairs={{0,6},{1,7},{2,0},{3,1},{4,2},{5,3},{6,4},{7,5},{8,14},{9,15},{10,... | collective-permute-start | bytes 1572872 | tf_op jit(solution)/shard_map/ppermute | solution.py:54
  43.1 13.2 %collective-permute-start.16 = (bf16[256,1024]{1,0:T(8,128)(2,1)S(1)}, bf16[256,1024]{1,0:T(8,128)(2,1)S(1)}, u32[]{:S(2)}, u32[]{:S(2)}) collective-permute-start(bf16[256,1024]{1,0:T(8,128)(2,1)S(1)} %pad_maximum_fusion.2), channel_id=1, source_target_pairs={{0,1},{1,0},{2,3},{3,2},{4,5},{5,4},{6,7},{7,6},{8,9},{9,8},{10,11... | collective-permute-start | bytes 1572872 | tf_op jit(solution)/shard_map/ppermute | solution.py:50
  44.4 6.6 %collective-permute-start.11 = (bf16[64,2048]{1,0:T(8,128)(2,1)S(1)}, bf16[64,2048]{1,0:T(8,128)(2,1)S(1)}, u32[]{:S(2)}, u32[]{:S(2)}) collective-permute-start(bf16[64,2048]{1,0:T(8,128)(2,1)S(1)} %slice.132), channel_id=1, source_target_pairs={{0,224},{8,40},{16,240},{24,56},{32,0},{40,72},{48,16},{56,88},{64... | collective-permute-start | bytes 786440 | tf_op jit(solution)/shard_map/ppermute | solution.py:42
  45.2 12.2 %collective-permute-start.14 = (bf16[128,2048]{1,0:T(8,128)(2,1)S(1)}, bf16[128,2048]{1,0:T(8,128)(2,1)S(1)}, u32[]{:S(2)}, u32[]{:S(2)}) collective-permute-start(bf16[128,2048]{1,0:T(8,128)(2,1)S(1)} %collective-permute-done.10.refs_10_), channel_id=1, source_target_pairs={{0,8},{8,0},{16,24},{24,16},{32,40},{40,32},{48,56},{56,48},{64,72... | collective-permute-start | bytes 1572872 | tf_op jit(solution)/shard_map/ppermute | solution.py:30
  51.1 6.3 %collective-permute-start.12 = (bf16[64,2048]{1,0:T(8,128)(2,1)S(1)}, bf16[64,2048]{1,0:T(8,128)(2,1)S(1)}, u32[]{:S(2)}, u32[]{:S(2)}) collective-permute-start(bf16[64,2048]{1,0:T(8,128)(2,1)S(1)} %collective-permute-done.11.refs_7_), channel_id=1, source_target_pairs={{0,8},{8,0},{16,24},{24,16},{32,40},{40,32},{48,56},{56,48},{64,72... | collective-permute-start | bytes 786440 | tf_op jit(solution)/shard_map/ppermute | solution.py:30
  78.4 6.8 %collective-permute-start.18 = (bf16[448,2048]{1,0:T(8,128)(2,1)S(1)}, bf16[448,2048]{1,0:T(8,128)(2,1)S(1)}, u32[]{:S(2)}, u32[]{:S(2)}) collective-permute-start(bf16[448,2048]{1,0:T(8,128)(2,1)S(1)} %get-tuple-element.35), channel_id=1, source_target_pairs={{0,8},{8,0},{16,24},{24,16},{32,40},{40,32},{48,56},{56,48},{64,72... | collective-permute-start | bytes 5505032 | tf_op jit(solution)/shard_map/ppermute | solution.py:30
  82.5 21.6 %collective-permute-start.22 = (bf16[256,1024]{1,0:T(8,128)(2,1)S(1)}, bf16[256,1024]{1,0:T(8,128)(2,1)S(1)}, u32[]{:S(2)}, u32[]{:S(2)}) collective-permute-start(bf16[256,1024]{1,0:T(8,128)(2,1)S(1)} %get-tuple-element.45), channel_id=1, source_target_pairs={{0,6},{1,7},{2,0},{3,1},{4,2},{5,3},{6,4},{7,5},{8,14},{9,15},{10,... | collective-permute-start | bytes 1572872 | tf_op jit(solution)/shard_map/ppermute | solution.py:54
  83.7 17.3 %collective-permute-start.23 = (bf16[256,1024]{1,0:T(8,128)(2,1)S(1)}, bf16[256,1024]{1,0:T(8,128)(2,1)S(1)}, u32[]{:S(2)}, u32[]{:S(2)}) collective-permute-start(bf16[256,1024]{1,0:T(8,128)(2,1)S(1)} %get-tuple-element.47), channel_id=1, source_target_pairs={{0,1},{1,0},{2,3},{3,2},{4,5},{5,4},{6,7},{7,6},{8,9},{9,8},{10,11... | collective-permute-start | bytes 1572872 | tf_op jit(solution)/shard_map/ppermute | solution.py:50
  85.0 19.1 %collective-permute-start.21 = (bf16[256,1024]{1,0:T(8,128)(2,1)S(1)}, bf16[256,1024]{1,0:T(8,128)(2,1)S(1)}, u32[]{:S(2)}, u32[]{:S(2)}) collective-permute-start(bf16[256,1024]{1,0:T(8,128)(2,1)S(1)} %get-tuple-element.42), channel_id=1, source_target_pairs={{0,2},{1,3},{2,4},{3,5},{4,6},{5,7},{6,0},{7,1},{8,10},{9,11},{10,... | collective-permute-start | bytes 1572872 | tf_op jit(solution)/shard_map/ppermute | solution.py:54
  85.3 7.6 %collective-permute-start.19 = (bf16[64,2048]{1,0:T(8,128)(2,1)S(1)}, bf16[64,2048]{1,0:T(8,128)(2,1)S(1)}, u32[]{:S(2)}, u32[]{:S(2)}) collective-permute-start(bf16[64,2048]{1,0:T(8,128)(2,1)S(1)} %add_convert_fusion.8), channel_id=1, source_target_pairs={{0,32},{8,232},{16,48},{24,248},{32,64},{40,8},{48,80},{56,24},{64... | collective-permute-start | bytes 786440 | tf_op jit(solution)/shard_map/ppermute | solution.py:46
  93.1 11.6 %collective-permute-start.20 = (bf16[128,2048]{1,0:T(8,128)(2,1)S(1)}, bf16[128,2048]{1,0:T(8,128)(2,1)S(1)}, u32[]{:S(2)}, u32[]{:S(2)}) collective-permute-start(bf16[128,2048]{1,0:T(8,128)(2,1)S(1)} %add_convert_fusion.6), channel_id=1, source_target_pairs={{0,32},{8,232},{16,48},{24,248},{32,64},{40,8},{48,80},{56,24},{64... | collective-permute-start | bytes 1572872 | tf_op jit(solution)/shard_map/ppermute | solution.py:46
  101.2 12.1 %collective-permute-start.25 = (bf16[128,1024]{1,0:T(8,128)(2,1)S(1)}, bf16[128,1024]{1,0:T(8,128)(2,1)S(1)}, u32[]{:S(2)}, u32[]{:S(2)}) collective-permute-start(bf16[128,1024]{1,0:T(8,128)(2,1)S(1)} %get-tuple-element.56), channel_id=1, source_target_pairs={{0,2},{1,3},{2,4},{3,5},{4,6},{5,7},{6,0},{7,1},{8,10},{9,11},{10,... | collective-permute-start | bytes 786440 | tf_op jit(solution)/shard_map/ppermute | solution.py:54
  101.3 8.4 %collective-permute-start.26 = (bf16[128,1024]{1,0:T(8,128)(2,1)S(1)}, bf16[128,1024]{1,0:T(8,128)(2,1)S(1)}, u32[]{:S(2)}, u32[]{:S(2)}) collective-permute-start(bf16[128,1024]{1,0:T(8,128)(2,1)S(1)} %get-tuple-element.57), channel_id=1, source_target_pairs={{0,6},{1,7},{2,0},{3,1},{4,2},{5,3},{6,4},{7,5},{8,14},{9,15},{10,... | collective-permute-start | bytes 786440 | tf_op jit(solution)/shard_map/ppermute | solution.py:54
  104.4 13.8 %collective-permute-start.30 = (bf16[256,1024]{1,0:T(8,128)(2,1)S(1)}, bf16[256,1024]{1,0:T(8,128)(2,1)S(1)}, u32[]{:S(2)}, u32[]{:S(2)}) collective-permute-start(bf16[256,1024]{1,0:T(8,128)(2,1)S(1)} %add_convert_fusion.5), channel_id=1, source_target_pairs={{0,1},{1,0},{2,3},{3,2},{4,5},{5,4},{6,7},{7,6},{8,9},{9,8},{10,11... | collective-permute-start | bytes 1572872 | tf_op jit(solution)/shard_map/ppermute | solution.py:50
  104.9 8.6 %collective-permute-start.24 = (bf16[128,2048]{1,0:T(8,128)(2,1)S(1)}, bf16[128,2048]{1,0:T(8,128)(2,1)S(1)}, u32[]{:S(2)}, u32[]{:S(2)}) collective-permute-start(bf16[128,2048]{1,0:T(8,128)(2,1)S(1)} %add_convert_fusion.3), channel_id=1, source_target_pairs={{0,32},{8,232},{16,48},{24,248},{32,64},{40,8},{48,80},{56,24},{64... | collective-permute-start | bytes 1572872 | tf_op jit(solution)/shard_map/ppermute | solution.py:46
  109.8 14.9 %collective-permute-start.29 = (bf16[256,1024]{1,0:T(8,128)(2,1)S(1)}, bf16[256,1024]{1,0:T(8,128)(2,1)S(1)}, u32[]{:S(2)}, u32[]{:S(2)}) collective-permute-start(bf16[256,1024]{1,0:T(8,128)(2,1)S(1)} %add_convert_fusion.1), channel_id=1, source_target_pairs={{0,6},{1,7},{2,0},{3,1},{4,2},{5,3},{6,4},{7,5},{8,14},{9,15},{10,... | collective-permute-start | bytes 1572872 | tf_op jit(solution)/shard_map/ppermute | solution.py:54
  113.4 14.6 %collective-permute-start.28 = (bf16[256,1024]{1,0:T(8,128)(2,1)S(1)}, bf16[256,1024]{1,0:T(8,128)(2,1)S(1)}, u32[]{:S(2)}, u32[]{:S(2)}) collective-permute-start(bf16[256,1024]{1,0:T(8,128)(2,1)S(1)} %add_convert_fusion.2), channel_id=1, source_target_pairs={{0,2},{1,3},{2,4},{3,5},{4,6},{5,7},{6,0},{7,1},{8,10},{9,11},{10,... | collective-permute-start | bytes 1572872 | tf_op jit(solution)/shard_map/ppermute | solution.py:54
  113.8 14.2 %collective-permute-start.27 = (bf16[128,2048]{1,0:T(8,128)(2,1)S(1)}, bf16[128,2048]{1,0:T(8,128)(2,1)S(1)}, u32[]{:S(2)}, u32[]{:S(2)}) collective-permute-start(bf16[128,2048]{1,0:T(8,128)(2,1)S(1)} %add_convert_fusion), channel_id=1, source_target_pairs={{0,32},{8,232},{16,48},{24,248},{32,64},{40,8},{48,80},{56,24},{64... | collective-permute-start | bytes 1572872 | tf_op jit(solution)/shard_map/ppermute | solution.py:46
  130.5 6.3 %collective-permute-start.32 = (bf16[32,2048]{1,0:T(8,128)(2,1)S(1)}, bf16[32,2048]{1,0:T(8,128)(2,1)S(1)}, u32[]{:S(2)}, u32[]{:S(2)}) collective-permute-start(bf16[32,2048]{1,0:T(8,128)(2,1)S(1)} %slice.206), channel_id=1, source_target_pairs={{0,16},{8,24},{16,0},{24,8},{32,48},{40,56},{48,32},{56,40},{64,80... | collective-permute-start | bytes 393224 | tf_op jit(solution)/shard_map/ppermute | solution.py:34
  (7 other events, 98.1 us)
